TPU v7x, 512 devices: a whole 4x4x16 slice. The times are simulated.
512 devices in a mesh: dp: 128 (over y, z_lo, x, core), tensor: 4 (over z_hi).
Axes of the slice: x: 4, y: 4, z: 16 (z_hi: 4, z_lo: 4; z = z_hi * 4 + z_lo), core: 2. Of those that a mesh axis runs over, the one named last changes fastest.
Arguments:
- queries: bfloat16 [16384, 2048], P('dp', 'tensor'), may hold values from -480 to 480
- encodings: bfloat16 [65536, 896], P('dp', 'tensor'), may hold values from -6 to 6
- kv_weight: bfloat16 [2, 896, 2048], P(None, None, 'tensor'), may hold values from -0.1875 to 0.1875
- w_out: bfloat16 [2048, 4096], P('tensor', 'dp'), may hold values from -0.5 to 0.5
- nbr_map: int32 [256, 16], P('dp'), may hold values from 0 to 4095, as said below
Outputs:
- attended: bfloat16 [16384, 4096], P('dp', 'tensor')
Inputs may be any that keep to these rules, and one draw needn't show every extreme that they name: `nbr_map`: an entry is shard * 32 + row block within that shard. Among the 32 entries of the 2 spans on one index of dp, each shard is named exactly 1 times or not at all.
All inputs are finite; a program needn't handle non-finite values.
Results may differ from a plain program's by a relative error of at most 0.014.
The roundings to bfloat16 on the way count: a program that leaves them out, or rounds other values in their place, can miss the bound.
Values may be sent and summed in bfloat16 or wider, within the bound.
No kernel may reach another device: no remote copies, remote signals or barrier semaphores. Data moves between devices by JAX's collectives and lax.ppermute only.
A program may use at most 64 MiB of HBM per device.

v0:
```python
import math

import jax
import jax.numpy as jnp
from jax import lax
from jax.sharding import PartitionSpec as P

HEAD = 128
SPAN = 64
ROWBLK = 16


def shards(queries, encodings, kv_weight, w_out, nbr_map):
    dp_count = lax.axis_size("dp")
    spans, per_span = nbr_map.shape
    requests = spans * per_span
    capacity = max(1, requests // dp_count)
    enc_blocks = encodings.shape[0] // ROWBLK
    head_width = queries.shape[1]
    head_count = head_width // HEAD
    flat_map = nbr_map.reshape(requests)
    source_shard = flat_map // enc_blocks
    row_block = flat_map % enc_blocks
    positions = jnp.arange(requests, dtype=jnp.int32)
    earlier = (source_shard[:, None] == source_shard[None, :]) & (
        positions[None, :] < positions[:, None]
    )
    slot_rank = jnp.sum(earlier.astype(jnp.int32), axis=1)
    recv_slot = source_shard * capacity + slot_rank
    slot_ids = jnp.arange(dp_count * capacity, dtype=jnp.int32)
    onehot_table = (recv_slot[:, None] == slot_ids[None, :]).astype(jnp.int32)
    wanted = jnp.sum(onehot_table * (row_block[:, None] + 1), axis=0) - 1
    incoming = lax.all_to_all(
        wanted.reshape(dp_count, capacity), "dp", split_axis=0, concat_axis=0, tiled=True
    )
    served = jnp.maximum(incoming, 0)
    is_live = (incoming >= 0)[:, :, None, None]
    all_features = lax.all_gather(encodings, "tensor", axis=1, tiled=True)
    key_rows = jnp.dot(all_features, kv_weight[0], preferred_element_type=jnp.float32).astype(
        jnp.bfloat16
    )
    value_rows = jnp.dot(all_features, kv_weight[1], preferred_element_type=jnp.float32).astype(
        jnp.bfloat16
    )
    key_rows, value_rows = (key_rows, value_rows)
    key_value = jnp.concatenate([key_rows, value_rows], axis=1).reshape(
        enc_blocks, ROWBLK, 2 * head_width
    )
    chosen = key_value[served]
    arrived = lax.all_to_all(
        jnp.where(is_live, chosen, jnp.zeros_like(chosen)),
        "dp",
        split_axis=0,
        concat_axis=0,
        tiled=True,
    )
    slots = arrived.reshape(dp_count * capacity, ROWBLK, arrived.shape[3])
    gathered = slots[recv_slot].reshape(spans, per_span * ROWBLK, arrived.shape[3])
    span_keys = gathered[:, :, :head_width]
    span_values = gathered[:, :, head_width:]
    query_heads = queries.reshape(spans, SPAN, head_count, HEAD)
    key_heads = span_keys.reshape(spans, -1, head_count, HEAD)
    value_heads = span_values.reshape(spans, -1, head_count, HEAD)
    scores = jnp.einsum(
        "cqhd,ckhd->chqk", query_heads, key_heads, preferred_element_type=jnp.float32
    )
    scores = scores * (1.0 / math.sqrt(HEAD))
    row_max = jnp.max(scores, axis=-1, keepdims=True)
    exponent = jnp.exp(scores - row_max)
    weights = (exponent / jnp.sum(exponent, axis=-1, keepdims=True)).astype(jnp.bfloat16)
    attn_mix = jnp.einsum(
        "chqk,ckhd->cqhd", weights, value_heads, preferred_element_type=jnp.float32
    )
    attn_mix = attn_mix.astype(jnp.bfloat16).reshape(spans * SPAN, head_width)
    partial_value = jnp.dot(
        attn_mix,
        lax.all_gather(w_out, "dp", axis=1, tiled=True),
        preferred_element_type=jnp.float32,
    )
    partial_value = partial_value.astype(jnp.bfloat16)
    partial_value = lax.optimization_barrier(partial_value).astype(jnp.float32)
    return lax.psum_scatter(
        partial_value.astype(jnp.bfloat16), "tensor", scatter_dimension=1, tiled=True
    )


def solution(mesh):
    return jax.shard_map(
        shards,
        mesh=mesh,
        in_specs=(
            P("dp", "tensor"),
            P("dp", "tensor"),
            P(None, None, "tensor"),
            P("tensor", "dp"),
            P("dp", None),
        ),
        out_specs=P("dp", "tensor"),
        check_vma=False,
    )
```

profile of v0, /device:TPU:1, one launch (start us, length us, event | category | flops | bytes accessed | tf_op | source)
XLA Modules:
  0.0 379.2 jit_solution(2861472818216291841)
XLA Ops:
  6.5 0.9 reshape.221
  7.7 0.7 copy.32
  8.5 13.8 %all-to-all-start = ((s32[128,1,1]{2,1,0:T(1,128)}), s32[128,1,1]{2,1,0:T(1,128)S(1)}, u32[]{:S(2)}, u32[]{:S(2)}) async-start(s32[128,1,1]{2,1,0:T(1,128)} %copy.32), calls=%async_computation | async-start | bytes 131072 | tf_op jit(solution)/shard_map/all_to_all | solution.py:33
  22.3 36.3 %all_gather.6 = bf16[512,896]{0,1:T(8,128)(2,1)S(1)} all-gather(bf16[512,224]{0,1:T(8,128)(2,1)} %param.6), channel_id=1, replica_groups=mesh['dp'=128,'tensor'=4] {'tensor'}, dimensions={1}, use_global_device_ids=true | all-gather | bytes 1146880 | tf_op jit(solution)/shard_map/all_gather | solution.py:38
  58.6 1.9 convolution_convert_fusion.1
  60.6 0.8 convolution_convert_fusion.2
  61.4 0.5 copy.33
  62.0 2.4 maximum_reduce_fusion
  64.3 2.8 gather_fusion
  67.1 2.4 compare_reduce_fusion
  69.5 4.5 %fusion.1 = bf16[128,1,16,1024]{3,2,1,0:T(8,128)(2,1)} fusion(bf16[128,16,1024]{2,1,0:T(8,128)(2,1)} %gather_fusion, pred[128]{0:T(512)(128)(4,1)S(1)} %compare_reduce_fusion), kind=kLoop, calls=%fused_computation.5 | loop fusion | flops 2097152 | bytes 8388736 | tf_op jit(solution)/shard_map/jit(_where)/select_n | solution.py:51
  74.0 18.6 %all-to-all-start.1 = ((bf16[128,1,16,1024]{3,2,1,0:T(8,128)(2,1)}), bf16[128,1,16,1024]{3,2,1,0:T(8,128)(2,1)}, u32[]{:S(2)}, u32[]{:S(2)}) async-start(bf16[128,1,16,1024]{3,2,1,0:T(8,128)(2,1)} %fusion.1), calls=%async_computation.1 | async-start | bytes 8388608 | tf_op jit(solution)/shard_map/all_to_all | solution.py:50
  92.7 0.7 all-gather.2.cloned.1.call-update
  93.4 0.2 reduce-scatter.2.cloned.1.call-start
  93.7 95.5 %all-to-all-done.1 = bf16[128,1,16,1024]{3,2,1,0:T(8,128)(2,1)} async-done(((bf16[128,1,16,1024]{3,2,1,0:T(8,128)(2,1)}), bf16[128,1,16,1024]{3,2,1,0:T(8,128)(2,1)}, u32[]{:S(2)}, u32[]{:S(2)}) %all-to-all-start.1) | async-done | bytes 4194336 | tf_op jit(solution)/shard_map/all_to_all | solution.py:50
  189.2 2.8 gather_fusion.1
  192.1 0.2 copy.36
  192.3 0.2 copy.35
  192.6 0.2 fusion.4
  192.8 0.3 fusion.19
  193.0 0.9 fusion.5
  194.1 116.8 %all-gather.2.cloned.1.call-done = bf16[512,4096]{0,1:T(8,128)(2,1)} async-done(((bf16[512,32]{0,1:T(8,128)(2,1)}), bf16[512,4096]{0,1:T(8,128)(2,1)}) %all-gather.2.cloned.1.call-update) | async-done | bytes 4194320 | tf_op jit(solution)/shard_map/all_gather | solution.py:77
  310.9 4.6 %convolution_convert_fusion = bf16[128,4096]{1,0:T(8,128)(2,1)} fusion(bf16[512,4096]{0,1:T(8,128)(2,1)} %all-gather.2.cloned.1.call-done, bf16[16,8,4,128]{3,2,1,0:T(4,128)(2,1)S(1)} %bitcast.45), kind=kOutput, calls=%fused_computation.3 | convolution fusion | flops 537395200 | bytes 5373952 | tf_op jit(solution)/shard_map/dot_general | solution.py:75
  315.6 56.7 %reduce-scatter.2.cloned.1.call-done = bf16[128,1024]{1,0:T(8,128)(2,1)} async-done(((bf16[128,4096]{1,0:T(8,128)(2,1)}), bf16[128,1024]{1,0:T(8,128)(2,1)}) %reduce-scatter.2.cloned.1.call-update) | async-done | bytes 262160 | tf_op jit(solution)/shard_map/reduce_scatter | solution.py:82
  (22 shorter events, 0.8 us)
Async XLA Ops:
  6.5 54.0 %copy-start.1 = (bf16[2,896,512]{2,1,0:T(8,128)(2,1)S(1)}, bf16[2,896,512]{2,1,0:T(8,128)(2,1)}, u32[]{:S(2)}) copy-start(bf16[2,896,512]{2,1,0:T(8,128)(2,1)} %param.7) | copy-start | bytes 5505028
  8.5 53.5 %all-to-all-start = ((s32[128,1,1]{2,1,0:T(1,128)}), s32[128,1,1]{2,1,0:T(1,128)S(1)}, u32[]{:S(2)}, u32[]{:S(2)}) async-start(s32[128,1,1]{2,1,0:T(1,128)} %copy.32), calls=%async_computation | async-start | bytes 131072 | tf_op jit(solution)/shard_map/all_to_all | solution.py:33
  74.0 19.6 %copy-start.2 = (s32[2,16]{1,0:T(2,128)S(1)}, s32[2,16]{1,0:T(2,128)}, u32[]{:S(2)}) copy-start(s32[2,16]{1,0:T(2,128)} %param.9) | copy-start | bytes 388
  74.0 19.7 %copy-start = (bf16[128,512]{1,0:T(8,128)(2,1)S(1)}, bf16[128,512]{1,0:T(8,128)(2,1)}, u32[]{:S(2)}) copy-start(bf16[128,512]{1,0:T(8,128)(2,1)} %param.5) | copy-start | bytes 393220
  74.0 115.2 %all-to-all-start.1 = ((bf16[128,1,16,1024]{3,2,1,0:T(8,128)(2,1)}), bf16[128,1,16,1024]{3,2,1,0:T(8,128)(2,1)}, u32[]{:S(2)}, u32[]{:S(2)}) async-start(bf16[128,1,16,1024]{3,2,1,0:T(8,128)(2,1)} %fusion.1), calls=%async_computation.1 | async-start | bytes 8388608 | tf_op jit(solution)/shard_map/all_to_all | solution.py:50
  92.6 218.3 %all-gather.2.cloned.1.call-start = ((), (), s32[]{:S(2)}) async-start(), calls=%async_computation.3 | async-start | bytes 4227072 | tf_op jit(solution)/shard_map/all_gather | solution.py:77
  93.4 279.0 %reduce-scatter.2.cloned.1.call-start = ((), (), s32[]{:S(2)}) async-start(), calls=%async_computation.4 | async-start | bytes 1310720 | tf_op jit(solution)/shard_map/reduce_scatter | solution.py:82
Sparse Core Ops, SparseCore 0:
  95.6 215.2 all-gather.1
  315.7 56.5 reduce-scatter.1
where the time goes:
time: 381 us; the launch traced here: 379 us
  waiting for transfers between devices  270 us (71%)
  blocking collectives  36.3 us (10%)
  starting transfers between devices  32.7 us (9%)
  between operations  13.6 us (4%)
  other arithmetic  9.88 us (3%)
  local copies, waits for them, and re-layouts  8.53 us (2%)
  matrix products  8.5 us (2%)
    all_gather x1, waiting for transfers between devices, shards(): lax.all_gather(w_out, 'dp', axis=1, tiled=True)  117 us
    all_to_all x1, waiting for transfers between devices, shards(): lax.all_to_all(jnp.where(is_live, chosen, jnp.zeros_like(chosen)), 'dp',...  95.5 us
    reduce_scatter x1, waiting for transfers between devices, shards(): lax.psum_scatter(partial_value.astype(jnp.bfloat16), 'tensor', scatter_di...  56.7 us
    all_gather x1, blocking collectives, shards(): all_features = lax.all_gather(encodings, 'tensor', axis=1, tiled=True)  36.3 us
    all_to_all x1, starting transfers between devices, shards(): lax.all_to_all(jnp.where(is_live, chosen, jnp.zeros_like(chosen)), 'dp',...  18.6 us
    all_to_all x1, starting transfers between devices, shards(): lax.all_to_all(wanted.reshape(dp_count, capacity), 'dp', split_axis=0, co...  13.8 us
  transfers between devices with their start and end apart: 4, of which 3 were waited for; matrix products, arithmetic and copies ran while one was open for 2% of the time, Pallas kernels for 0%

commit v1 on v0

v1 whole, which is shorter than its diff:
```python
import functools
import math

import jax
import jax.numpy as jnp
from jax import lax
from jax.experimental import pallas as pl
from jax.experimental.pallas import tpu as pltpu
from jax.sharding import Mesh
from jax.sharding import PartitionSpec as P

HEAD = 128
SPAN = 64
ROWBLK = 16
NY, NZ, NX, NC, NT = 4, 4, 4, 2, 4
DP = ("y", "z", "x", "c")
LAST_DIMS = (((1,), (1,)), ((), ()))


def attend_kernel(q_ref, feat_ref, kv_ref, mixed_ref):
    spans = q_ref.shape[0] // SPAN
    per_span = feat_ref.shape[1] // spans
    heads = q_ref.shape[1] // HEAD
    feats = feat_ref[...].T
    keys = jnp.dot(feats, kv_ref[0], preferred_element_type=jnp.float32)
    keys = keys.astype(jnp.bfloat16)
    values = jnp.dot(feats, kv_ref[1], preferred_element_type=jnp.float32)
    values = values.astype(jnp.bfloat16)
    for span in range(spans):
        for head in range(heads):
            tokens = slice(span * SPAN, (span + 1) * SPAN)
            rows = slice(span * per_span, (span + 1) * per_span)
            lanes = slice(head * HEAD, (head + 1) * HEAD)
            scores = lax.dot_general(
                q_ref[tokens, lanes], keys[rows, lanes], LAST_DIMS,
                preferred_element_type=jnp.float32,
            ) * (1.0 / math.sqrt(HEAD))
            exponent = jnp.exp(scores - jnp.max(scores, axis=-1, keepdims=True))
            weights = exponent / jnp.sum(exponent, axis=-1, keepdims=True)
            mixed = jnp.dot(
                weights.astype(jnp.bfloat16), values[rows, lanes],
                preferred_element_type=jnp.float32,
            )
            mixed_ref[tokens, lanes] = mixed.astype(jnp.bfloat16)


def attend(queries, feats, kv_weight):
    return pl.pallas_call(
        attend_kernel,
        out_shape=jax.ShapeDtypeStruct(queries.shape, jnp.bfloat16),
        compiler_params=pltpu.CompilerParams(vmem_limit_bytes=32 * 2**20),
        name="attend",
    )(queries, feats, kv_weight)


def project_kernel(mixed_ref, w_ref, out_ref):
    total = None
    for group in range(mixed_ref.shape[0]):
        partial = lax.dot_general(
            mixed_ref[group], w_ref[0, group], LAST_DIMS,
            preferred_element_type=jnp.float32,
        )
        partial = partial.astype(jnp.bfloat16).astype(jnp.float32)
        total = partial if total is None else total + partial
    out_ref[...] = total.astype(jnp.bfloat16)


def project(mixed, w_cols):
    groups, tokens, width = mixed.shape
    blocks, _, cols, _ = w_cols.shape
    return pl.pallas_call(
        project_kernel,
        grid=(blocks,),
        in_specs=[
            pl.BlockSpec((groups, tokens, width), lambda i: (0, 0, 0)),
            pl.BlockSpec((1, groups, cols, width), lambda i: (i, 0, 0, 0)),
        ],
        out_specs=pl.BlockSpec((tokens, cols), lambda i: (0, i)),
        out_shape=jax.ShapeDtypeStruct((tokens, blocks * cols), jnp.bfloat16),
        compiler_params=pltpu.CompilerParams(vmem_limit_bytes=32 * 2**20),
        name="project",
    )(mixed, w_cols)


def device_index(y, z, x, c, t):
    return (((y * NZ + z) * NX + x) * NC + c) * NT + t


def to_column_owner():
    pairs = []
    for y in range(NY):
        for block in range(NZ * NX * NC):
            z, x, c = block // (NX * NC), block // NC % NX, block % NC
            xc, new_z = block // NZ, block % NZ
            for t in range(NT):
                target = device_index(t, new_z, xc // NC, xc % NC, y)
                pairs.append((device_index(y, z, x, c, t), target))
    return pairs


def shards(queries, encodings, kv_weight, w_out, nbr_map):
    dp_count = lax.axis_size(DP)
    enc_blocks = encodings.shape[0] // ROWBLK
    features = encodings.shape[1]
    flat_map = nbr_map.reshape(-1)
    source_shard = flat_map // enc_blocks
    row_block = flat_map % enc_blocks

    shard_ids = jnp.arange(dp_count, dtype=jnp.int32)
    wanted = jnp.sum(
        jnp.where(source_shard[:, None] == shard_ids[None, :], row_block[:, None], 0), axis=0
    )
    served = lax.all_to_all(
        wanted.reshape(dp_count, 1), DP, split_axis=0, concat_axis=0, tiled=True
    ).reshape(dp_count)

    piece = lax.ppermute(w_out.T, DP + ("t",), to_column_owner())
    piece = lax.all_gather(piece, "z", axis=0, tiled=True)
    w_cols = lax.all_gather(piece, ("x", "c", "y"), axis=0, tiled=True)
    w_cols = w_cols.reshape(NX * NC, NY, piece.shape[0], piece.shape[1])

    chosen = encodings.reshape(enc_blocks, ROWBLK, features)[served]
    arrived = lax.all_to_all(chosen, DP, split_axis=0, concat_axis=0, tiled=True)
    gathered = arrived[source_shard].reshape(-1, features).T
    feats = lax.all_gather(gathered, "t", axis=0, tiled=True)

    mixed = attend(queries, feats, kv_weight)
    mixed = lax.all_gather(mixed, "t", axis=0, tiled=False)
    return project(mixed, w_cols)


def solution(mesh):
    fine = Mesh(mesh.devices.reshape(NY, NZ, NX, NC, NT), DP + ("t",))
    return jax.shard_map(
        shards,
        mesh=fine,
        in_specs=(
            P(DP, "t"),
            P(DP, "t"),
            P(None, None, "t"),
            P("t", DP),
            P(DP, None),
        ),
        out_specs=P(DP, "t"),
        check_vma=False,
    )
```

time: 381 us -> 188 us (0.49)
  waiting for transfers between devices: 270 us -> 41.1 us
  blocking collectives: 36.3 us -> 82.4 us
  matrix products: 8.5 us -> 0 us
  Pallas kernels: 0 us -> 7.56 us
  other arithmetic: 9.88 us -> 2.5 us
    all_gather x1, waiting for transfers between devices: 117 us -> 0.01 us  [shards(): w_cols = lax.all_gather(piece, ('x', 'c', 'y'), axis=0, tiled=True)]
    all_to_all x2, waiting for transfers between devices: 95.5 us -> 38.2 us  [the longest x1 29.5 us: shards(): lax.all_to_all(chosen, DP, split_axis=0, concat_axis=0, tiled=True)]
    reduce_scatter x1 -> x0, waiting for transfers between devices: 56.7 us -> none  [shards(): lax.psum_scatter(partial_value.astype(jnp.bfloat16), 'tensor', scatter_di...]
    all_gather x1 -> x3, blocking collectives: 36.3 us -> 82.4 us  [the longest x1 41.3 us: shards(): feats = lax.all_gather(gathered, 't', axis=0, tiled=True)]
    dot_general x5 -> x0, matrix products: 8.5 us -> none  [the longest x1 4.65 us: shards(): jnp.dot(attn_mix, lax.all_gather(w_out, 'dp', axis=1, tiled=True), prefer...]
    pallas_call x0 -> x2, Pallas kernels: none -> 7.56 us  [the longest x1 4.01 us: project(): pl.pallas_call(project_kernel, grid=(blocks,), in_specs=[pl.BlockSpec((gr...]
    ppermute x0 -> x1, starting transfers between devices: none -> 5.06 us  [shards(): piece = lax.ppermute(w_out.T, DP + ('t',), to_column_owner())]
    select_n x2, other arithmetic: 4.54 us -> 0.02 us  [the longest x1 0.01 us: shards(): gathered = arrived[source_shard].reshape(-1, features).T]
  transfers between devices with their start and end apart: 4 -> 4, of which waited for: 3 -> 3; matrix products, arithmetic and copies ran while one was open for 2% -> 4% of each run, Pallas kernels for 0% -> 2%
where the time goes in v1:
time: 188 us; the launch traced here: 187 us
  blocking collectives  82.4 us (44%)
  waiting for transfers between devices  41.1 us (22%)
  starting transfers between devices  33.1 us (18%)
  between operations  13.5 us (7%)
  Pallas kernels  7.56 us (4%)
  local copies, waits for them, and re-layouts  7.17 us (4%)
  other arithmetic  2.5 us (1%)
    all_gather x1, blocking collectives, shards(): feats = lax.all_gather(gathered, 't', axis=0, tiled=True)  41.3 us
    all_to_all x1, waiting for transfers between devices, shards(): lax.all_to_all(chosen, DP, split_axis=0, concat_axis=0, tiled=True)  29.5 us
    all_gather x1, blocking collectives, shards(): mixed = lax.all_gather(mixed, 't', axis=0, tiled=False)  24.2 us
    all_to_all x1, starting transfers between devices, shards(): lax.all_to_all(wanted.reshape(dp_count, 1), DP, split_axis=0, concat_axis...  21.8 us
    all_gather x1, blocking collectives, shards(): piece = lax.all_gather(piece, 'z', axis=0, tiled=True)  17 us
    all_to_all x1, waiting for transfers between devices, shards(): lax.all_to_all(wanted.reshape(dp_count, 1), DP, split_axis=0, concat_axis...  8.63 us
    all_to_all x1, starting transfers between devices, shards(): lax.all_to_all(chosen, DP, split_axis=0, concat_axis=0, tiled=True)  6.18 us
    ppermute x1, starting transfers between devices, shards(): piece = lax.ppermute(w_out.T, DP + ('t',), to_column_owner())  5.06 us
  transfers between devices with their start and end apart: 4, of which 3 were waited for; matrix products, arithmetic and copies ran while one was open for 4% of the time, Pallas kernels for 2%

profile of v1, /device:TPU:1, one launch (start us, length us, event | category | flops | bytes accessed | tf_op | source)
XLA Modules:
  0.0 187.3 jit_solution(12934725548218637575)
XLA Ops:
  6.5 0.0 all-gather.3.cloned.1.call-start
  6.5 5.1 %collective-permute-start = (bf16[32,512]{1,0:T(8,128)(2,1)}, bf16[32,512]{1,0:T(8,128)(2,1)S(1)}, u32[]{:S(2)}, u32[]{:S(2)}) collective-permute-start(bf16[32,512]{1,0:T(8,128)(2,1)} %bitcast.19), channel_id=1, source_target_pairs={{0,0},{1,128},{2,256},{3,384},{4,32},{5,160},{6,288},{7,416},{8,64... | collective-permute-start | bytes 98312 | tf_op jit(solution)/shard_map/ppermute | solution.py:117
  11.6 2.9 %collective-permute-done = bf16[32,512]{1,0:T(8,128)(2,1)S(1)} collective-permute-done((bf16[32,512]{1,0:T(8,128)(2,1)}, bf16[32,512]{1,0:T(8,128)(2,1)S(1)}, u32[]{:S(2)}, u32[]{:S(2)}) %collective-permute-start) | collective-permute-done | bytes 32800 | tf_op jit(solution)/shard_map/ppermute | solution.py:117
  14.5 17.0 %all_gather.18 = bf16[128,512]{1,0:T(8,128)(2,1)} all-gather(bf16[32,512]{1,0:T(8,128)(2,1)S(1)} %collective-permute-done), channel_id=1, replica_groups=mesh['y'=4,'z'=4,'x'=4,'c'=2,'t'=4] {'z'}, dimensions={0}, use_global_device_ids=true | all-gather | bytes 163840 | tf_op jit(solution)/shard_map/all_gather | solution.py:118
  31.5 0.0 all-gather.3.cloned.1.call-update
  31.5 0.8 reshape.156
  32.3 0.1 select_reduce_fusion
  32.4 0.7 copy.15
  33.1 21.8 %all-to-all-start = ((s32[128,1,1]{2,1,0:T(1,128)}), s32[128,1,1]{2,1,0:T(1,128)S(1)}, u32[]{:S(2)}, u32[]{:S(2)}) async-start(s32[128,1,1]{2,1,0:T(1,128)} %copy.15), calls=%async_computation | async-start | bytes 131072 | tf_op jit(solution)/shard_map/all_to_all | solution.py:113
  55.0 1.1 copy.14
  56.0 8.6 %all-to-all-done = s32[128,1,1]{2,1,0:T(1,128)S(1)} async-done(((s32[128,1,1]{2,1,0:T(1,128)}), s32[128,1,1]{2,1,0:T(1,128)S(1)}, u32[]{:S(2)}, u32[]{:S(2)}) %all-to-all-start) | async-done | bytes 544 | tf_op jit(solution)/shard_map/all_to_all | solution.py:113
  64.7 2.4 %reduce = s32[128]{0:T(128)S(1)} reduce(s32[128,1,1]{2,1,0:T(1,128)S(1)} %all-to-all-done, s32[]{:T(128)} %constant.28.clone.1), dimensions={1,2}, to_apply=%all_to_all.12.reduce_sub_computation | reduce | bytes 1028 | tf_op jit(solution)/shard_map/all_to_all | solution.py:113
  67.1 1.6 gather_fusion
  68.7 6.2 %all-to-all-start.1 = ((bf16[128,16,224]{2,1,0:T(8,128)(2,1)}), bf16[128,16,224]{2,1,0:T(8,128)(2,1)S(1)}, u32[]{:S(2)}, u32[]{:S(2)}) async-start(bf16[128,16,224]{2,1,0:T(8,128)(2,1)} %gather_fusion), calls=%async_computation.1 | async-start | bytes 2097152 | tf_op jit(solution)/shard_map/all_to_all | solution.py:123
  74.8 0.0 copy-done.3
  74.9 0.1 reshape.157
  75.0 29.5 %all-to-all-done.1 = bf16[128,16,224]{2,1,0:T(8,128)(2,1)S(1)} async-done(((bf16[128,16,224]{2,1,0:T(8,128)(2,1)}), bf16[128,16,224]{2,1,0:T(8,128)(2,1)S(1)}, u32[]{:S(2)}, u32[]{:S(2)}) %all-to-all-start.1) | async-done | bytes 917536 | tf_op jit(solution)/shard_map/all_to_all | solution.py:123
  104.5 0.6 gather_fusion.1
  105.1 0.1 copy.16
  105.2 41.3 %all_gather.15.feat_ref = bf16[896,512]{1,0:T(8,128)(2,1)S(1)} all-gather(bf16[224,512]{1,0:T(8,128)(2,1)S(1)} %bitcast.17), channel_id=1, replica_groups=mesh['y'=4,'z'=4,'x'=4,'c'=2,'t'=4] {'t'}, dimensions={0}, use_global_device_ids=true | all-gather | bytes 1146880 | tf_op jit(solution)/shard_map/all_gather | solution.py:125
  146.5 3.6 %attend.1 = bf16[128,512]{1,0:T(8,128)(2,1)S(1)} custom-call(bf16[128,512]{1,0:T(8,128)(2,1)S(1)} %copy-done.2, bf16[896,512]{1,0:T(8,128)(2,1)S(1)} %all_gather.15.feat_ref, bf16[2,896,512]{2,1,0:T(8,128)(2,1)S(1)} %copy-done.1), custom_call_target="tpu_custom_call" | custom-call | tf_op jit(solution)/shard_map/attend/pallas_call | solution.py:48
  150.1 24.2 %all-gather = bf16[512,512]{1,0:T(8,128)(2,1)S(1)} all-gather(bf16[128,512]{1,0:T(8,128)(2,1)S(1)} %attend.1), channel_id=2, replica_groups=mesh['y'=4,'z'=4,'x'=4,'c'=2,'t'=4] {'t'}, dimensions={0}, use_global_device_ids=true | all-gather | bytes 655360 | tf_op jit(solution)/shard_map/all_gather | solution.py:128
  174.2 2.2 %copy-done = bf16[4096,512]{1,0:T(8,128)(2,1)S(1)} copy-done((bf16[4096,512]{1,0:T(8,128)(2,1)S(1)}, bf16[4096,512]{1,0:T(8,128)(2,1)}, u32[]{:S(2)}) %copy-start) | copy-done | bytes 4194328
  176.4 4.0 %project.1 = bf16[128,1024]{1,0:T(8,128)(2,1)} custom-call(bf16[4,128,512]{2,1,0:T(8,128)(2,1)S(1)} %bitcast.14, bf16[8,4,128,512]{3,2,1,0:T(8,128)(2,1)S(1)} %bitcast.13), custom_call_target="tpu_custom_call" | custom-call | tf_op jit(solution)/shard_map/project/pallas_call | solution.py:71
  (12 shorter events, 0.1 us)
Async XLA Ops:
  6.5 68.3 %copy-start.3 = (s32[2,16]{1,0:T(2,128)S(1)}, s32[2,16]{1,0:T(2,128)}, u32[]{:S(2)}) copy-start(s32[2,16]{1,0:T(2,128)} %param.9) | copy-start | bytes 388
  6.5 140.0 %copy-start.2 = (bf16[128,512]{1,0:T(8,128)(2,1)S(1)}, bf16[128,512]{1,0:T(8,128)(2,1)}, u32[]{:S(2)}) copy-start(bf16[128,512]{1,0:T(8,128)(2,1)} %q_ref.1) | copy-start | bytes 393220
  6.5 140.0 %copy-start.1 = (bf16[2,896,512]{2,1,0:T(8,128)(2,1)S(1)}, bf16[2,896,512]{2,1,0:T(8,128)(2,1)}, u32[]{:S(2)}) copy-start(bf16[2,896,512]{2,1,0:T(8,128)(2,1)} %kv_ref.1) | copy-start | bytes 5505028
  6.5 167.7 %all-gather.3.cloned.1.call-start = ((), (), s32[]{:S(2)}) async-start(), calls=%async_computation.2 | async-start | bytes 4325376 | tf_op jit(solution)/shard_map/all_gather | solution.py:119
  6.5 8.0 %collective-permute-start = (bf16[32,512]{1,0:T(8,128)(2,1)}, bf16[32,512]{1,0:T(8,128)(2,1)S(1)}, u32[]{:S(2)}, u32[]{:S(2)}) collective-permute-start(bf16[32,512]{1,0:T(8,128)(2,1)} %bitcast.19), channel_id=1, source_target_pairs={{0,0},{1,128},{2,256},{3,384},{4,32},{5,160},{6,288},{7,416},{8,64... | collective-permute-start | bytes 98312 | tf_op jit(solution)/shard_map/ppermute | solution.py:117
  33.1 31.5 %all-to-all-start = ((s32[128,1,1]{2,1,0:T(1,128)}), s32[128,1,1]{2,1,0:T(1,128)S(1)}, u32[]{:S(2)}, u32[]{:S(2)}) async-start(s32[128,1,1]{2,1,0:T(1,128)} %copy.15), calls=%async_computation | async-start | bytes 131072 | tf_op jit(solution)/shard_map/all_to_all | solution.py:113
  68.7 35.8 %all-to-all-start.1 = ((bf16[128,16,224]{2,1,0:T(8,128)(2,1)}), bf16[128,16,224]{2,1,0:T(8,128)(2,1)S(1)}, u32[]{:S(2)}, u32[]{:S(2)}) async-start(bf16[128,16,224]{2,1,0:T(8,128)(2,1)} %gather_fusion), calls=%async_computation.1 | async-start | bytes 2097152 | tf_op jit(solution)/shard_map/all_to_all | solution.py:123
  174.2 2.2 %copy-start = (bf16[4096,512]{1,0:T(8,128)(2,1)S(1)}, bf16[4096,512]{1,0:T(8,128)(2,1)}, u32[]{:S(2)}) copy-start(bf16[4096,512]{1,0:T(8,128)(2,1)} %all-gather.3.cloned.1.call-done) | copy-start | bytes 12582916
Sparse Core Ops, SparseCore 0:
  31.6 74.2 all-gather.2

commit v2 on v1

--- a/solution.py
+++ b/solution.py
@@ -14,6 +14,7 @@
 ROWBLK = 16
 NY, NZ, NX, NC, NT = 4, 4, 4, 2, 4
 DP = ("y", "z", "x", "c")
+PEERS = ("y", "x", "c")
 LAST_DIMS = (((1,), (1,)), ((), ()))
 
 
@@ -53,12 +54,71 @@
     )(queries, feats, kv_weight)
 
 
+def pick_kernel(served_ref, feats_ref, piece_ref, chosen_ref, piece_out_ref, rows_ref):
+    shards_here, _, rows = feats_ref.shape
+    for z in range(shards_here):
+        rows_ref[z * rows : (z + 1) * rows] = feats_ref[z].T
+    for peer in range(chosen_ref.shape[0]):
+        for z in range(shards_here):
+            start = pl.multiple_of(served_ref[peer, 0, z] * ROWBLK, ROWBLK)
+            chosen_ref[peer, z] = rows_ref[pl.ds(z * rows + start, ROWBLK)]
+    piece_out_ref[...] = piece_ref[...]
+
+
+def pick(served, feats, piece):
+    shards_here, features, rows = feats.shape
+    return pl.pallas_call(
+        pick_kernel,
+        in_specs=[
+            pl.BlockSpec(memory_space=pltpu.SMEM),
+            pl.BlockSpec(memory_space=pltpu.VMEM),
+            pl.BlockSpec(memory_space=pltpu.VMEM),
+        ],
+        out_shape=(
+            jax.ShapeDtypeStruct(
+                (served.shape[0], shards_here, ROWBLK, features), feats.dtype
+            ),
+            jax.ShapeDtypeStruct(piece.shape, piece.dtype),
+        ),
+        scratch_shapes=[pltpu.VMEM((shards_here * rows, features), feats.dtype)],
+        compiler_params=pltpu.CompilerParams(vmem_limit_bytes=32 * 2**20),
+        name="pick",
+    )(served, feats, piece)
+
+
+def take_kernel(slot_ref, arrived_ref, four_ref, feats_ref, four_out_ref, rows_ref):
+    for at in range(slot_ref.shape[0]):
+        rows_ref[at * ROWBLK : (at + 1) * ROWBLK] = arrived_ref[slot_ref[at]]
+    feats_ref[...] = rows_ref[...].T
+    four_out_ref[...] = four_ref[...]
+
+
+def take(slots, arrived, four):
+    rows, features = slots.shape[0] * ROWBLK, arrived.shape[2]
+    return pl.pallas_call(
+        take_kernel,
+        in_specs=[
+            pl.BlockSpec(memory_space=pltpu.SMEM),
+            pl.BlockSpec(memory_space=pltpu.VMEM),
+            pl.BlockSpec(memory_space=pltpu.VMEM),
+        ],
+        out_shape=(
+            jax.ShapeDtypeStruct((features, rows), arrived.dtype),
+            jax.ShapeDtypeStruct(four.shape, four.dtype),
+        ),
+        scratch_shapes=[pltpu.VMEM((rows, features), arrived.dtype)],
+        compiler_params=pltpu.CompilerParams(vmem_limit_bytes=32 * 2**20),
+        name="take",
+    )(slots, arrived, four)
+
+
 def project_kernel(mixed_ref, w_ref, out_ref):
+    places, groups, _, cols, width = w_ref.shape
     total = None
-    for group in range(mixed_ref.shape[0]):
+    for group in range(groups):
         partial = lax.dot_general(
-            mixed_ref[group], w_ref[0, group], LAST_DIMS,
-            preferred_element_type=jnp.float32,
+            mixed_ref[group], w_ref[:, group, 0].reshape(places * cols, width),
+            LAST_DIMS, preferred_element_type=jnp.float32,
         )
         partial = partial.astype(jnp.bfloat16).astype(jnp.float32)
         total = partial if total is None else total + partial
@@ -67,17 +127,17 @@
 
 def project(mixed, w_cols):
     groups, tokens, width = mixed.shape
-    blocks, _, cols, _ = w_cols.shape
+    places, _, blocks, cols, _ = w_cols.shape
     return pl.pallas_call(
         project_kernel,
         grid=(blocks,),
         in_specs=[
             pl.BlockSpec((groups, tokens, width), lambda i: (0, 0, 0)),
-            pl.BlockSpec((1, groups, cols, width), lambda i: (i, 0, 0, 0)),
+            pl.BlockSpec((places, groups, 1, cols, width), lambda i: (0, 0, i, 0, 0)),
         ],
-        out_specs=pl.BlockSpec((tokens, cols), lambda i: (0, i)),
-        out_shape=jax.ShapeDtypeStruct((tokens, blocks * cols), jnp.bfloat16),
-        compiler_params=pltpu.CompilerParams(vmem_limit_bytes=32 * 2**20),
+        out_specs=pl.BlockSpec((tokens, places * cols), lambda i: (0, i)),
+        out_shape=jax.ShapeDtypeStruct((tokens, places * blocks * cols), jnp.bfloat16),
+        compiler_params=pltpu.CompilerParams(vmem_limit_bytes=60 * 2**20),
         name="project",
     )(mixed, w_cols)
 
@@ -87,41 +147,41 @@
 
 
 def to_column_owner():
-    pairs = []
-    for y in range(NY):
-        for block in range(NZ * NX * NC):
-            z, x, c = block // (NX * NC), block // NC % NX, block % NC
-            xc, new_z = block // NZ, block % NZ
-            for t in range(NT):
-                target = device_index(t, new_z, xc // NC, xc % NC, y)
-                pairs.append((device_index(y, z, x, c, t), target))
-    return pairs
+    return [
+        (device_index(y, z, x, c, t), device_index(t, z, x, c, y))
+        for y in range(NY) for z in range(NZ) for x in range(NX) for c in range(NC)
+        for t in range(NT)
+    ]
 
 
 def shards(queries, encodings, kv_weight, w_out, nbr_map):
-    dp_count = lax.axis_size(DP)
     enc_blocks = encodings.shape[0] // ROWBLK
-    features = encodings.shape[1]
     flat_map = nbr_map.reshape(-1)
-    source_shard = flat_map // enc_blocks
+    shard = flat_map // enc_blocks
     row_block = flat_map % enc_blocks
-
-    shard_ids = jnp.arange(dp_count, dtype=jnp.int32)
+    peer = shard // (NZ * NX * NC) * (NX * NC) + shard % (NX * NC)
+    slots = peer * NZ + shard // (NX * NC) % NZ
+
+    lanes = jnp.arange(NY * NX * NC * 128, dtype=jnp.int32)
+    lane_slot = jnp.where(lanes % 128 < NZ, lanes // 128 * NZ + lanes % 128, -1)
     wanted = jnp.sum(
-        jnp.where(source_shard[:, None] == shard_ids[None, :], row_block[:, None], 0), axis=0
+        jnp.where(slots[:, None] == lane_slot[None, :], row_block[:, None], 0), axis=0
     )
     served = lax.all_to_all(
-        wanted.reshape(dp_count, 1), DP, split_axis=0, concat_axis=0, tiled=True
-    ).reshape(dp_count)
+        wanted.reshape(NY * NX * NC, 1, 128), PEERS, split_axis=0, concat_axis=0, tiled=True
+    )
+    enc_z = lax.all_gather(encodings.T, "z", axis=0, tiled=False)
 
     piece = lax.ppermute(w_out.T, DP + ("t",), to_column_owner())
-    piece = lax.all_gather(piece, "z", axis=0, tiled=True)
-    w_cols = lax.all_gather(piece, ("x", "c", "y"), axis=0, tiled=True)
-    w_cols = w_cols.reshape(NX * NC, NY, piece.shape[0], piece.shape[1])
-
-    chosen = encodings.reshape(enc_blocks, ROWBLK, features)[served]
-    arrived = lax.all_to_all(chosen, DP, split_axis=0, concat_axis=0, tiled=True)
-    gathered = arrived[source_shard].reshape(-1, features).T
+
+    chosen, piece = pick(served, enc_z, piece)
+    arrived = lax.all_to_all(chosen, PEERS, split_axis=0, concat_axis=0, tiled=True)
+    arrived = arrived.reshape(-1, ROWBLK, encodings.shape[1])
+    four = lax.all_gather(piece, "z", axis=0, tiled=True)
+
+    gathered, four = take(slots, arrived, four)
+    w_cols = lax.all_gather(four, ("x", "c", "y"), axis=0, tiled=True)
+    w_cols = w_cols.reshape(NX * NC, NY, NZ, w_out.shape[1], w_out.shape[0])
     feats = lax.all_gather(gathered, "t", axis=0, tiled=True)
 
     mixed = attend(queries, feats, kv_weight)

time: 188 us -> 156 us (0.83)
  waiting for transfers between devices: 41.1 us -> 5.86 us
  blocking collectives: 82.4 us -> 91.2 us
  local copies, waits for them, and re-layouts: 7.17 us -> 1.87 us
  Pallas kernels: 7.56 us -> 11 us
  starting transfers between devices: 33.1 us -> 30.4 us
    all_to_all x2, waiting for transfers between devices: 38.2 us -> 5.83 us  [the longest x1 5.83 us: shards(): lax.all_to_all(chosen, PEERS, split_axis=0, concat_axis=0, tiled=True)]
    all_gather x1 -> x2, blocking collectives: 17 us -> 32.5 us  [the longest x1 21.2 us: shards(): enc_z = lax.all_gather(encodings.T, 'z', axis=0, tiled=False)]
    all_gather x1, blocking collectives: 41.3 us -> 36.7 us  [shards(): feats = lax.all_gather(gathered, 't', axis=0, tiled=True)]
    ppermute x1, starting transfers between devices: 5.06 us -> 1.42 us  [shards(): piece = lax.ppermute(w_out.T, DP + ('t',), to_column_owner())]
    ppermute x1, waiting for transfers between devices: 2.9 us -> 0.01 us  [shards(): piece = lax.ppermute(w_out.T, DP + ('t',), to_column_owner())]
    pallas_call x0 -> x2, Pallas kernels: none -> 2.53 us  [the longest x1 1.28 us: pick(): pl.pallas_call(pick_kernel, in_specs=[pl.BlockSpec(memory_space=pltpu.SME...]
    all_to_all x1 -> x0, other arithmetic: 2.36 us -> none  [shards(): lax.all_to_all(wanted.reshape(dp_count, 1), DP, split_axis=0, concat_axis...]
    unnamed x9 -> x6, local copies, waits for them, and re-layouts: 3.27 us -> 0.97 us
  transfers between devices with their start and end apart: 4 -> 4, of which waited for: 3 -> 1; matrix products, arithmetic and copies ran while one was open for 4% -> 0% of each run, Pallas kernels for 2% -> 2%
where the time goes in v2:
time: 156 us; the launch traced here: 155 us
  blocking collectives  91.2 us (58%)
  starting transfers between devices  30.4 us (19%)
  between operations  13.4 us (9%)
  Pallas kernels  11 us (7%)
  waiting for transfers between devices  5.86 us (4%)
  local copies, waits for them, and re-layouts  1.87 us (1%)
    all_gather x1, blocking collectives, shards(): feats = lax.all_gather(gathered, 't', axis=0, tiled=True)  36.7 us
    all_gather x1, blocking collectives, shards(): mixed = lax.all_gather(mixed, 't', axis=0, tiled=False)  22 us
    all_gather x1, blocking collectives, shards(): enc_z = lax.all_gather(encodings.T, 'z', axis=0, tiled=False)  21.2 us
    all_to_all x1, starting transfers between devices, shards(): lax.all_to_all(chosen, PEERS, split_axis=0, concat_axis=0, tiled=True)  18.6 us
    all_gather x1, blocking collectives, shards(): four = lax.all_gather(piece, 'z', axis=0, tiled=True)  11.3 us
    all_to_all x1, starting transfers between devices, shards(): lax.all_to_all(wanted.reshape(NY * NX * NC, 1, 128), PEERS, split_axis=0,...  10.4 us
    all_to_all x1, waiting for transfers between devices, shards(): lax.all_to_all(chosen, PEERS, split_axis=0, concat_axis=0, tiled=True)  5.83 us
    pallas_call x1, Pallas kernels, project(): pl.pallas_call(project_kernel, grid=(blocks,), in_specs=[pl.BlockSpec((gr...  4.89 us
  transfers between devices with their start and end apart: 4, of which 1 were waited for; matrix products, arithmetic and copies ran while one was open for 0% of the time, Pallas kernels for 2%

profile of v2, /device:TPU:1, one launch (start us, length us, event | category | flops | bytes accessed | tf_op | source)
XLA Modules:
  0.0 154.6 jit_solution(5866789885845516571)
XLA Ops:
  6.5 0.0 copy-start
  6.5 0.9 reshape.136
  7.5 0.8 select_reduce_fusion
  8.2 10.4 %all-to-all-start = ((s32[32,1,128]{2,1,0:T(1,128)}), s32[32,1,128]{2,1,0:T(1,128)S(1)}, u32[]{:S(2)}, u32[]{:S(2)}) async-start(s32[32,1,128]{2,1,0:T(1,128)} %bitcast), calls=%async_computation | async-start | bytes 32768 | tf_op jit(solution)/shard_map/all_to_all | solution.py:170
  18.6 1.4 collective-permute-start
  20.0 21.2 %all-gather = bf16[896,512]{1,0:T(8,128)(2,1)S(1)} all-gather(bf16[224,512]{1,0:T(8,128)(2,1)} %bitcast.11), channel_id=2, replica_groups=mesh['y'=4,'z'=4,'x'=4,'c'=2,'t'=4] {'z'}, dimensions={0}, use_global_device_ids=true | all-gather | bytes 1146880 | tf_op jit(solution)/shard_map/all_gather | solution.py:173
  41.2 0.0 all-to-all-done.served_ref
  41.2 0.0 collective-permute-done.piece_ref
  41.2 1.3 pick.1
  42.5 0.0 copy-start.1
  42.5 1.0 copy-done.1
  43.5 18.6 %all-to-all-start.1 = ((bf16[32,4,16,224]{3,2,1,0:T(8,128)(2,1)}), bf16[32,4,16,224]{3,2,1,0:T(8,128)(2,1)S(1)}, u32[]{:S(2)}, u32[]{:S(2)}) async-start(bf16[32,4,16,224]{3,2,1,0:T(8,128)(2,1)} %copy-done.1), calls=%async_computation.1 | async-start | bytes 2097152 | tf_op jit(solution)/shard_map/all_to_all | solution.py:178
  62.1 0.0 all-gather.4.cloned.1.call-start
  62.1 11.3 %all_gather.23.four_ref = bf16[128,512]{1,0:T(8,128)(2,1)S(1)} all-gather(bf16[32,512]{1,0:T(8,128)(2,1)S(1)} %get-tuple-element.10), channel_id=1, replica_groups=mesh['y'=4,'z'=4,'x'=4,'c'=2,'t'=4] {'z'}, dimensions={0}, use_global_device_ids=true | all-gather | bytes 163840 | tf_op jit(solution)/shard_map/all_gather | solution.py:180
  73.4 5.8 %all-to-all-done.1 = bf16[32,4,16,224]{3,2,1,0:T(8,128)(2,1)S(1)} async-done(((bf16[32,4,16,224]{3,2,1,0:T(8,128)(2,1)}), bf16[32,4,16,224]{3,2,1,0:T(8,128)(2,1)S(1)}, u32[]{:S(2)}, u32[]{:S(2)}) %all-to-all-start.1) | async-done | bytes 917536 | tf_op jit(solution)/shard_map/all_to_all | solution.py:178
  79.2 1.3 take.1
  80.5 0.0 all-gather.4.cloned.1.call-update
  80.5 36.7 %all_gather.24.feat_ref = bf16[896,512]{1,0:T(8,128)(2,1)S(1)} all-gather(bf16[224,512]{1,0:T(8,128)(2,1)S(1)} %get-tuple-element.11), channel_id=1, replica_groups=mesh['y'=4,'z'=4,'x'=4,'c'=2,'t'=4] {'t'}, dimensions={0}, use_global_device_ids=true | all-gather | bytes 1146880 | tf_op jit(solution)/shard_map/all_gather | solution.py:185
  117.2 0.0 copy-done.2
  117.2 0.0 copy-done
  117.2 3.6 %attend.1 = bf16[128,512]{1,0:T(8,128)(2,1)S(1)} custom-call(bf16[128,512]{1,0:T(8,128)(2,1)S(1)} %copy-done.2, bf16[896,512]{1,0:T(8,128)(2,1)S(1)} %all_gather.24.feat_ref, bf16[2,896,512]{2,1,0:T(8,128)(2,1)S(1)} %copy-done), custom_call_target="tpu_custom_call" | custom-call | tf_op jit(solution)/shard_map/attend/pallas_call | solution.py:49
  120.8 22.0 %all-gather.1 = bf16[512,512]{1,0:T(8,128)(2,1)} all-gather(bf16[128,512]{1,0:T(8,128)(2,1)S(1)} %attend.1), channel_id=3, replica_groups=mesh['y'=4,'z'=4,'x'=4,'c'=2,'t'=4] {'t'}, dimensions={0}, use_global_device_ids=true | all-gather | bytes 655360 | tf_op jit(solution)/shard_map/all_gather | solution.py:188
  142.8 0.0 all-gather.4.cloned.1.call-done
  142.8 4.9 %project.1 = bf16[128,1024]{1,0:T(8,128)(2,1)} custom-call(bf16[4,128,512]{2,1,0:T(8,128)(2,1)} %bitcast.10, bf16[8,4,4,32,512]{4,3,2,1,0:T(8,128)(2,1)} %bitcast.9), custom_call_target="tpu_custom_call" | custom-call | tf_op jit(solution)/shard_map/project/pallas_call | solution.py:131
  (3 shorter events, 0.0 us)
Async XLA Ops:
  6.5 110.7 %copy-start.2 = (bf16[128,512]{1,0:T(8,128)(2,1)S(1)}, bf16[128,512]{1,0:T(8,128)(2,1)}, u32[]{:S(2)}) copy-start(bf16[128,512]{1,0:T(8,128)(2,1)} %q_ref.1) | copy-start | bytes 393220
  6.5 110.7 %copy-start = (bf16[2,896,512]{2,1,0:T(8,128)(2,1)S(1)}, bf16[2,896,512]{2,1,0:T(8,128)(2,1)}, u32[]{:S(2)}) copy-start(bf16[2,896,512]{2,1,0:T(8,128)(2,1)} %kv_ref.1) | copy-start | bytes 5505028
  8.2 33.0 %all-to-all-start = ((s32[32,1,128]{2,1,0:T(1,128)}), s32[32,1,128]{2,1,0:T(1,128)S(1)}, u32[]{:S(2)}, u32[]{:S(2)}) async-start(s32[32,1,128]{2,1,0:T(1,128)} %bitcast), calls=%async_computation | async-start | bytes 32768 | tf_op jit(solution)/shard_map/all_to_all | solution.py:170
  18.6 22.6 %collective-permute-start = (bf16[32,512]{1,0:T(8,128)(2,1)}, bf16[32,512]{1,0:T(8,128)(2,1)S(1)}, u32[]{:S(2)}, u32[]{:S(2)}) collective-permute-start(bf16[32,512]{1,0:T(8,128)(2,1)} %bitcast.12), channel_id=1, source_target_pairs={{0,0},{1,128},{2,256},{3,384},{4,4},{5,132},{6,260},{7,388},{8,8},... | collective-permute-start | bytes 98312 | tf_op jit(solution)/shard_map/ppermute | solution.py:175
  42.5 1.0 copy-start.1
  43.5 35.7 %all-to-all-start.1 = ((bf16[32,4,16,224]{3,2,1,0:T(8,128)(2,1)}), bf16[32,4,16,224]{3,2,1,0:T(8,128)(2,1)S(1)}, u32[]{:S(2)}, u32[]{:S(2)}) async-start(bf16[32,4,16,224]{3,2,1,0:T(8,128)(2,1)} %copy-done.1), calls=%async_computation.1 | async-start | bytes 2097152 | tf_op jit(solution)/shard_map/all_to_all | solution.py:178
  62.1 80.8 %all-gather.4.cloned.1.call-start = ((), (), s32[]{:S(2)}) async-start(), calls=%async_computation.2 | async-start | bytes 4325376 | tf_op jit(solution)/shard_map/all_gather | solution.py:183
Sparse Core Ops, SparseCore 0:
  80.6 52.8 all-gather.3

commit v3 on v2

--- a/solution.py
+++ b/solution.py
@@ -18,7 +18,8 @@
 LAST_DIMS = (((1,), (1,)), ((), ()))
 
 
-def attend_kernel(q_ref, feat_ref, kv_ref, mixed_ref):
+def attend_kernel(q_ref, feat_ref, kv_ref, cols_ref, mixed_ref, cols_out_ref):
+    del cols_ref, cols_out_ref
     spans = q_ref.shape[0] // SPAN
     per_span = feat_ref.shape[1] // spans
     heads = q_ref.shape[1] // HEAD
@@ -45,13 +46,20 @@
             mixed_ref[tokens, lanes] = mixed.astype(jnp.bfloat16)
 
 
-def attend(queries, feats, kv_weight):
+def attend(queries, feats, kv_weight, cols):
+    in_vmem, anywhere = pl.BlockSpec(memory_space=pltpu.VMEM), pl.BlockSpec(memory_space=pl.ANY)
     return pl.pallas_call(
         attend_kernel,
-        out_shape=jax.ShapeDtypeStruct(queries.shape, jnp.bfloat16),
+        in_specs=[in_vmem, in_vmem, in_vmem, anywhere],
+        out_specs=(in_vmem, anywhere),
+        out_shape=(
+            jax.ShapeDtypeStruct(queries.shape, jnp.bfloat16),
+            jax.ShapeDtypeStruct(cols.shape, cols.dtype),
+        ),
+        input_output_aliases={3: 1},
         compiler_params=pltpu.CompilerParams(vmem_limit_bytes=32 * 2**20),
         name="attend",
-    )(queries, feats, kv_weight)
+    )(queries, feats, kv_weight, cols)
 
 
 def pick_kernel(served_ref, feats_ref, piece_ref, chosen_ref, piece_out_ref, rows_ref):
@@ -86,60 +94,63 @@
     )(served, feats, piece)
 
 
-def take_kernel(slot_ref, arrived_ref, four_ref, feats_ref, four_out_ref, rows_ref):
+def take_kernel(slot_ref, arrived_ref, pieces_ref, feats_ref, pieces_out_ref, rows_ref):
+    del pieces_ref, pieces_out_ref
     for at in range(slot_ref.shape[0]):
         rows_ref[at * ROWBLK : (at + 1) * ROWBLK] = arrived_ref[slot_ref[at]]
     feats_ref[...] = rows_ref[...].T
-    four_out_ref[...] = four_ref[...]
-
-
-def take(slots, arrived, four):
+
+
+def take(slots, arrived, pieces):
     rows, features = slots.shape[0] * ROWBLK, arrived.shape[2]
     return pl.pallas_call(
         take_kernel,
         in_specs=[
             pl.BlockSpec(memory_space=pltpu.SMEM),
             pl.BlockSpec(memory_space=pltpu.VMEM),
-            pl.BlockSpec(memory_space=pltpu.VMEM),
+            pl.BlockSpec(memory_space=pl.ANY),
         ],
+        out_specs=(
+            pl.BlockSpec(memory_space=pltpu.VMEM),
+            pl.BlockSpec(memory_space=pl.ANY),
+        ),
         out_shape=(
             jax.ShapeDtypeStruct((features, rows), arrived.dtype),
-            jax.ShapeDtypeStruct(four.shape, four.dtype),
-        ),
+            jax.ShapeDtypeStruct(pieces.shape, pieces.dtype),
+        ),
+        input_output_aliases={2: 1},
         scratch_shapes=[pltpu.VMEM((rows, features), arrived.dtype)],
         compiler_params=pltpu.CompilerParams(vmem_limit_bytes=32 * 2**20),
         name="take",
-    )(slots, arrived, four)
-
-
-def project_kernel(mixed_ref, w_ref, out_ref):
-    places, groups, _, cols, width = w_ref.shape
-    total = None
-    for group in range(groups):
-        partial = lax.dot_general(
-            mixed_ref[group], w_ref[:, group, 0].reshape(places * cols, width),
-            LAST_DIMS, preferred_element_type=jnp.float32,
-        )
-        partial = partial.astype(jnp.bfloat16).astype(jnp.float32)
-        total = partial if total is None else total + partial
-    out_ref[...] = total.astype(jnp.bfloat16)
-
-
-def project(mixed, w_cols):
-    groups, tokens, width = mixed.shape
-    places, _, blocks, cols, _ = w_cols.shape
+    )(slots, arrived, pieces)
+
+
+def project_kernel(core_ref, mixed_ref, own_ref, other_ref, out_ref):
+    groups, cols, _ = own_ref.shape
+    step = 256
+    for half, w_ref in ((core_ref[0], own_ref), (1 - core_ref[0], other_ref)):
+        for col in range(0, cols, step):
+            total = None
+            for group in range(groups):
+                partial = lax.dot_general(
+                    mixed_ref[group], w_ref[group, col : col + step], LAST_DIMS,
+                    preferred_element_type=jnp.float32,
+                )
+                partial = partial.astype(jnp.bfloat16).astype(jnp.float32)
+                total = partial if total is None else total + partial
+            start = pl.multiple_of(half * cols + col, step)
+            out_ref[:, pl.ds(start, step)] = total.astype(jnp.bfloat16)
+
+
+def project(core, mixed, own, other):
     return pl.pallas_call(
         project_kernel,
-        grid=(blocks,),
-        in_specs=[
-            pl.BlockSpec((groups, tokens, width), lambda i: (0, 0, 0)),
-            pl.BlockSpec((places, groups, 1, cols, width), lambda i: (0, 0, i, 0, 0)),
-        ],
-        out_specs=pl.BlockSpec((tokens, places * cols), lambda i: (0, i)),
-        out_shape=jax.ShapeDtypeStruct((tokens, places * blocks * cols), jnp.bfloat16),
-        compiler_params=pltpu.CompilerParams(vmem_limit_bytes=60 * 2**20),
+        in_specs=[pl.BlockSpec(memory_space=pltpu.SMEM)]
+        + [pl.BlockSpec(memory_space=pltpu.VMEM)] * 3,
+        out_shape=jax.ShapeDtypeStruct((mixed.shape[1], NC * own.shape[1]), jnp.bfloat16),
+        compiler_params=pltpu.CompilerParams(vmem_limit_bytes=32 * 2**20),
         name="project",
-    )(mixed, w_cols)
+    )(core, mixed, own, other)
 
 
 def device_index(y, z, x, c, t):
@@ -147,11 +158,15 @@
 
 
 def to_column_owner():
-    return [
-        (device_index(y, z, x, c, t), device_index(t, z, x, c, y))
-        for y in range(NY) for z in range(NZ) for x in range(NX) for c in range(NC)
-        for t in range(NT)
-    ]
+    pairs = []
+    for y in range(NY):
+        for block in range(NZ * NX * NC):
+            z, x, c = block // (NX * NC), block // NC % NX, block % NC
+            new_c, new_x, new_z = block // (NX * NZ), block // NZ % NX, block % NZ
+            for t in range(NT):
+                target = device_index(t, new_z, new_x, new_c, y)
+                pairs.append((device_index(y, z, x, c, t), target))
+    return pairs
 
 
 def shards(queries, encodings, kv_weight, w_out, nbr_map):
@@ -178,15 +193,18 @@
     arrived = lax.all_to_all(chosen, PEERS, split_axis=0, concat_axis=0, tiled=True)
     arrived = arrived.reshape(-1, ROWBLK, encodings.shape[1])
     four = lax.all_gather(piece, "z", axis=0, tiled=True)
+    four = jnp.broadcast_to(four[None], (NY * NX,) + four.shape)
 
     gathered, four = take(slots, arrived, four)
-    w_cols = lax.all_gather(four, ("x", "c", "y"), axis=0, tiled=True)
-    w_cols = w_cols.reshape(NX * NC, NY, NZ, w_out.shape[1], w_out.shape[0])
+    own = lax.all_to_all(four, ("y", "x"), split_axis=0, concat_axis=0, tiled=True)
+    own = own.reshape(NY, -1, own.shape[2])
     feats = lax.all_gather(gathered, "t", axis=0, tiled=True)
 
-    mixed = attend(queries, feats, kv_weight)
+    mixed, own = attend(queries, feats, kv_weight, own)
+    other = lax.ppermute(own, "c", [(0, 1), (1, 0)])
     mixed = lax.all_gather(mixed, "t", axis=0, tiled=False)
-    return project(mixed, w_cols)
+    core = lax.axis_index("c").astype(jnp.int32).reshape(1)
+    return project(core, mixed, own, other)
 
 
 def solution(mesh):

time: 156 us -> 154 us (0.987)
  between operations: 13.4 us -> 0.09 us
  blocking collectives: 91.2 us -> 98 us
  starting transfers between devices: 30.4 us -> 34.4 us
  local copies, waits for them, and re-layouts: 1.87 us -> 3.78 us
    all_to_all x0 -> x1, starting transfers between devices: none -> 3.85 us  [shards(): lax.all_to_all(four, ('y', 'x'), split_axis=0, concat_axis=0, tiled=True)]
    all_gather x1, blocking collectives: 22 us -> 25.3 us  [shards(): mixed = lax.all_gather(mixed, 't', axis=0, tiled=False)]
    all_to_all x1, starting transfers between devices: 18.6 us -> 16 us  [shards(): lax.all_to_all(chosen, PEERS, split_axis=0, concat_axis=0, tiled=True)]
    ppermute x0 -> x1, starting transfers between devices: none -> 2.3 us  [shards(): other = lax.ppermute(own, 'c', [(0, 1), (1, 0)])]
    all_gather x1, blocking collectives: 36.7 us -> 38.6 us  [shards(): feats = lax.all_gather(gathered, 't', axis=0, tiled=True)]
    unnamed x6, local copies, waits for them, and re-layouts: 0.97 us -> 2.83 us
  transfers between devices with their start and end apart: 4 -> 5, of which waited for: 1 -> 1; matrix products, arithmetic and copies ran while one was open for 0% -> 0% of each run, Pallas kernels for 2% -> 0%
where the time goes in v3:
time: 154 us; the launch traced here: 153 us
  blocking collectives  98 us (64%)
  starting transfers between devices  34.4 us (22%)
  Pallas kernels  10.2 us (7%)
  waiting for transfers between devices  5.84 us (4%)
  local copies, waits for them, and re-layouts  3.78 us (2%)
    all_gather x1, blocking collectives, shards(): feats = lax.all_gather(gathered, 't', axis=0, tiled=True)  38.6 us
    all_gather x1, blocking collectives, shards(): mixed = lax.all_gather(mixed, 't', axis=0, tiled=False)  25.3 us
    all_gather x1, blocking collectives, shards(): enc_z = lax.all_gather(encodings.T, 'z', axis=0, tiled=False)  22.8 us
    all_to_all x1, starting transfers between devices, shards(): lax.all_to_all(chosen, PEERS, split_axis=0, concat_axis=0, tiled=True)  16 us
    all_gather x1, blocking collectives, shards(): four = lax.all_gather(piece, 'z', axis=0, tiled=True)  11.3 us
    all_to_all x1, starting transfers between devices, shards(): lax.all_to_all(wanted.reshape(NY * NX * NC, 1, 128), PEERS, split_axis=0,...  10.4 us
    all_to_all x1, waiting for transfers between devices, shards(): lax.all_to_all(chosen, PEERS, split_axis=0, concat_axis=0, tiled=True)  5.83 us
    all_to_all x1, starting transfers between devices, shards(): lax.all_to_all(four, ('y', 'x'), split_axis=0, concat_axis=0, tiled=True)  3.85 us
  transfers between devices with their start and end apart: 5, of which 1 were waited for; matrix products, arithmetic and copies ran while one was open for 0% of the time, Pallas kernels for 0%

profile of v3, /device:TPU:1, one launch (start us, length us, event | category | flops | bytes accessed | tf_op | source)
XLA Modules:
  0.0 153.2 jit_solution(7449136661431522549)
XLA Ops:
  0.0 0.8 reshape.141
  0.8 0.8 select_reduce_fusion
  1.6 10.4 %all-to-all-start = ((s32[32,1,128]{2,1,0:T(1,128)}), s32[32,1,128]{2,1,0:T(1,128)S(1)}, u32[]{:S(2)}, u32[]{:S(2)}) async-start(s32[32,1,128]{2,1,0:T(1,128)} %bitcast.1), calls=%async_computation | async-start | bytes 32768 | tf_op jit(solution)/shard_map/all_to_all | solution.py:185
  11.9 1.9 %collective-permute-start = (bf16[32,512]{1,0:T(8,128)(2,1)}, bf16[32,512]{1,0:T(8,128)(2,1)S(1)}, u32[]{:S(2)}, u32[]{:S(2)}) collective-permute-start(bf16[32,512]{1,0:T(8,128)(2,1)} %bitcast.13), channel_id=1, source_target_pairs={{0,0},{1,128},{2,256},{3,384},{4,32},{5,160},{6,288},{7,416},{8,64... | collective-permute-start | bytes 98312 | tf_op jit(solution)/shard_map/ppermute | solution.py:190
  13.8 22.8 %all-gather = bf16[896,512]{1,0:T(8,128)(2,1)S(1)} all-gather(bf16[224,512]{1,0:T(8,128)(2,1)} %bitcast.12), channel_id=2, replica_groups=mesh['y'=4,'z'=4,'x'=4,'c'=2,'t'=4] {'z'}, dimensions={0}, use_global_device_ids=true | all-gather | bytes 1146880 | tf_op jit(solution)/shard_map/all_gather | solution.py:188
  36.6 0.0 all-to-all-done.served_ref
  36.6 0.0 collective-permute-done.piece_ref
  36.6 2.2 %pick.1 = (bf16[32,4,16,224]{3,2,1,0:T(8,128)(2,1)}, bf16[32,512]{1,0:T(8,128)(2,1)S(1)}) custom-call(s32[32,1,128]{2,1,0:T(1,128)S(1)} %all-to-all-done.served_ref, bf16[4,224,512]{2,1,0:T(8,128)(2,1)S(1)} %bitcast.10, bf16[32,512]{1,0:T(8,128)(2,1)S(1)} %collective-permute-done.piece_ref), custom_call_target="tpu_custom_call" | custom-call | tf_op jit(solution)/shard_map/pick/pallas_call | solution.py:78
  38.9 16.0 %all-to-all-start.1 = ((bf16[32,4,16,224]{3,2,1,0:T(8,128)(2,1)}), bf16[32,4,16,224]{3,2,1,0:T(8,128)(2,1)S(1)}, u32[]{:S(2)}, u32[]{:S(2)}) async-start(bf16[32,4,16,224]{3,2,1,0:T(8,128)(2,1)} %get-tuple-element.11), calls=%async_computation.1 | async-start | bytes 2097152 | tf_op jit(solution)/shard_map/all_to_all | solution.py:193
  54.9 11.3 %all_gather.20 = bf16[128,512]{1,0:T(8,128)(2,1)S(1)} all-gather(bf16[32,512]{1,0:T(8,128)(2,1)S(1)} %get-tuple-element.12), channel_id=1, replica_groups=mesh['y'=4,'z'=4,'x'=4,'c'=2,'t'=4] {'z'}, dimensions={0}, use_global_device_ids=true | all-gather | bytes 163840 | tf_op jit(solution)/shard_map/all_gather | solution.py:195
  66.2 5.8 %all-to-all-done.1 = bf16[32,4,16,224]{3,2,1,0:T(8,128)(2,1)S(1)} async-done(((bf16[32,4,16,224]{3,2,1,0:T(8,128)(2,1)}), bf16[32,4,16,224]{3,2,1,0:T(8,128)(2,1)S(1)}, u32[]{:S(2)}, u32[]{:S(2)}) %all-to-all-start.1) | async-done | bytes 917536 | tf_op jit(solution)/shard_map/all_to_all | solution.py:193
  72.1 0.2 broadcast_in_dim.25.pieces_ref
  72.3 0.7 take.1
  72.9 0.0 copy-start
  72.9 1.3 copy-done
  74.3 3.8 %all-to-all-start.2 = ((bf16[16,128,512]{2,1,0:T(8,128)(2,1)}), bf16[16,128,512]{2,1,0:T(8,128)(2,1)S(1)}, u32[]{:S(2)}, u32[]{:S(2)}) async-start(bf16[16,128,512]{2,1,0:T(8,128)(2,1)} %copy-done), calls=%async_computation.2 | async-start | bytes 4194304 | tf_op jit(solution)/shard_map/all_to_all | solution.py:199
  78.1 38.6 %all_gather.21.feat_ref = bf16[896,512]{1,0:T(8,128)(2,1)S(1)} all-gather(bf16[224,512]{1,0:T(8,128)(2,1)S(1)} %get-tuple-element.13), channel_id=1, replica_groups=mesh['y'=4,'z'=4,'x'=4,'c'=2,'t'=4] {'t'}, dimensions={0}, use_global_device_ids=true | all-gather | bytes 1146880 | tf_op jit(solution)/shard_map/all_gather | solution.py:201
  116.7 0.0 all-to-all-done.2
  116.7 1.5 copy-done.1
  118.2 3.6 %attend.1 = (bf16[128,512]{1,0:T(8,128)(2,1)S(1)}, bf16[4,512,512]{2,1,0:T(8,128)(2,1)S(1)}) custom-call(bf16[128,512]{1,0:T(8,128)(2,1)S(1)} %copy-done.2, bf16[896,512]{1,0:T(8,128)(2,1)S(1)} %all_gather.21.feat_ref, bf16[2,896,512]{2,1,0:T(8,128)(2,1)S(1)} %copy-done.1, bf16[4,512,512]{2,1,0:T(8,128)(2,1)S(1)} %bitcast.8), custom_call_target="tpu_custom_call", output_to_operand_aliasing={{1}: (3, {})} | custom-call | tf_op jit(solution)/shard_map/attend/pallas_call | solution.py:51
  121.8 2.3 %collective-permute-start.1 = (bf16[4,512,512]{2,1,0:T(8,128)(2,1)S(1)}, bf16[4,512,512]{2,1,0:T(8,128)(2,1)}, u32[]{:S(2)}, u32[]{:S(2)}) collective-permute-start(bf16[4,512,512]{2,1,0:T(8,128)(2,1)S(1)} %get-tuple-element.16.own_ref), channel_id=1, source_target_pairs={{0,4},{4,0},{1,5},{5,1},{2,6},{6,2},{3,7},{7,3},{8,12},{12,8},{9,1... | collective-permute-start | bytes 6291464 | tf_op jit(solution)/shard_map/ppermute | solution.py:204
  124.1 25.3 %all-gather.1 = bf16[512,512]{1,0:T(8,128)(2,1)S(1)} all-gather(bf16[128,512]{1,0:T(8,128)(2,1)S(1)} %get-tuple-element.15), channel_id=3, replica_groups=mesh['y'=4,'z'=4,'x'=4,'c'=2,'t'=4] {'t'}, dimensions={0}, use_global_device_ids=true | all-gather | bytes 655360 | tf_op jit(solution)/shard_map/all_gather | solution.py:205
  149.4 0.0 collective-permute-done.1.other_ref
  149.4 3.8 %project.1 = bf16[128,1024]{1,0:T(8,128)(2,1)} custom-call(s32[1]{0:T(128)} %bitcast.core_ref, bf16[4,128,512]{2,1,0:T(8,128)(2,1)S(1)} %bitcast.11, bf16[4,512,512]{2,1,0:T(8,128)(2,1)S(1)} %get-tuple-element.16.own_ref, bf16[4,512,512]{2,1,0:T(8,128)(2,1)} %collective-permute-done.1.other_ref), custom_call_target="tpu_custom_call" | custom-call | tf_op jit(solution)/shard_map/project/pallas_call | solution.py:146
  (5 shorter events, 0.0 us)
Async XLA Ops:
  1.6 35.1 %all-to-all-start = ((s32[32,1,128]{2,1,0:T(1,128)}), s32[32,1,128]{2,1,0:T(1,128)S(1)}, u32[]{:S(2)}, u32[]{:S(2)}) async-start(s32[32,1,128]{2,1,0:T(1,128)} %bitcast.1), calls=%async_computation | async-start | bytes 32768 | tf_op jit(solution)/shard_map/all_to_all | solution.py:185
  11.9 24.7 %collective-permute-start = (bf16[32,512]{1,0:T(8,128)(2,1)}, bf16[32,512]{1,0:T(8,128)(2,1)S(1)}, u32[]{:S(2)}, u32[]{:S(2)}) collective-permute-start(bf16[32,512]{1,0:T(8,128)(2,1)} %bitcast.13), channel_id=1, source_target_pairs={{0,0},{1,128},{2,256},{3,384},{4,32},{5,160},{6,288},{7,416},{8,64... | collective-permute-start | bytes 98312 | tf_op jit(solution)/shard_map/ppermute | solution.py:190
  38.9 33.2 %all-to-all-start.1 = ((bf16[32,4,16,224]{3,2,1,0:T(8,128)(2,1)}), bf16[32,4,16,224]{3,2,1,0:T(8,128)(2,1)S(1)}, u32[]{:S(2)}, u32[]{:S(2)}) async-start(bf16[32,4,16,224]{3,2,1,0:T(8,128)(2,1)} %get-tuple-element.11), calls=%async_computation.1 | async-start | bytes 2097152 | tf_op jit(solution)/shard_map/all_to_all | solution.py:193
  72.9 1.3 copy-start
  74.3 42.4 %copy-start.2 = (bf16[128,512]{1,0:T(8,128)(2,1)S(1)}, bf16[128,512]{1,0:T(8,128)(2,1)}, u32[]{:S(2)}) copy-start(bf16[128,512]{1,0:T(8,128)(2,1)} %q_ref.1) | copy-start | bytes 393220
  74.3 42.4 %all-to-all-start.2 = ((bf16[16,128,512]{2,1,0:T(8,128)(2,1)}), bf16[16,128,512]{2,1,0:T(8,128)(2,1)S(1)}, u32[]{:S(2)}, u32[]{:S(2)}) async-start(bf16[16,128,512]{2,1,0:T(8,128)(2,1)} %copy-done), calls=%async_computation.2 | async-start | bytes 4194304 | tf_op jit(solution)/shard_map/all_to_all | solution.py:199
  116.7 1.5 copy-start.1
  121.8 27.6 %collective-permute-start.1 = (bf16[4,512,512]{2,1,0:T(8,128)(2,1)S(1)}, bf16[4,512,512]{2,1,0:T(8,128)(2,1)}, u32[]{:S(2)}, u32[]{:S(2)}) collective-permute-start(bf16[4,512,512]{2,1,0:T(8,128)(2,1)S(1)} %get-tuple-element.16.own_ref), channel_id=1, source_target_pairs={{0,4},{4,0},{1,5},{5,1},{2,6},{6,2},{3,7},{7,3},{8,12},{12,8},{9,1... | collective-permute-start | bytes 6291464 | tf_op jit(solution)/shard_map/ppermute | solution.py:204

commit v4 on v1

v4 whole, which is shorter than its diff:
```python
import math

import jax
import jax.numpy as jnp
from jax import lax
from jax.experimental import pallas as pl
from jax.experimental.pallas import tpu as pltpu
from jax.sharding import Mesh
from jax.sharding import PartitionSpec as P

HEAD = 128
SPAN = 64
ROWBLK = 16
LANES = 128
W_PARTS = 2
NY, NZ, NX, NC, NT = 4, 4, 4, 2, 4
DP = ("y", "z", "x", "c")
PEERS = ("y", "x", "c")
LAST_DIMS = (((1,), (1,)), ((), ()))
IN_SMEM = pl.BlockSpec(memory_space=pltpu.SMEM)
IN_VMEM = pl.BlockSpec(memory_space=pltpu.VMEM)
IN_HBM = pl.BlockSpec(memory_space=pltpu.HBM)
ANYWHERE = pl.BlockSpec(memory_space=pl.ANY)
PARAMS = pltpu.CompilerParams(vmem_limit_bytes=24 * 2**20)


def like(value):
    return jax.ShapeDtypeStruct(value.shape, value.dtype)


def slot_of(shard):
    per_y = NZ * NX * NC
    peer = shard // per_y * (NX * NC) + shard % (NX * NC)
    return peer * NZ + shard // (NX * NC) % NZ


def want(nbr_map, enc_blocks):
    blocks = nbr_map.astype(jnp.uint32)
    lane = jnp.arange(LANES, dtype=jnp.uint32)[None, :]
    code = jnp.arange(NY * NX * NC, dtype=jnp.uint32)[:, None] * NZ + lane
    code = jnp.where(lane < NZ, code, NY * NX * NC * NZ)
    here = slot_of(blocks // enc_blocks)[:, :, None, None] == code
    wanted = jnp.where(here, (blocks % enc_blocks)[:, :, None, None], 0)
    return jnp.sum(wanted, axis=(0, 1)).astype(jnp.int32)[:, None, :]


def attend_kernel(q_ref, feat_ref, kv_ref, mixed_ref):
    spans = q_ref.shape[0] // SPAN
    per_span = feat_ref.shape[1] // spans
    heads = q_ref.shape[1] // HEAD
    feats = feat_ref[...].T
    keys = jnp.dot(feats, kv_ref[0], preferred_element_type=jnp.float32)
    keys = keys.astype(jnp.bfloat16)
    values = jnp.dot(feats, kv_ref[1], preferred_element_type=jnp.float32)
    values = values.astype(jnp.bfloat16)
    for span in range(spans):
        for head in range(heads):
            tokens = slice(span * SPAN, (span + 1) * SPAN)
            rows = slice(span * per_span, (span + 1) * per_span)
            lanes = slice(head * HEAD, (head + 1) * HEAD)
            scores = lax.dot_general(
                q_ref[tokens, lanes], keys[rows, lanes], LAST_DIMS,
                preferred_element_type=jnp.float32,
            ) * (1.0 / math.sqrt(HEAD))
            exponent = jnp.exp(scores - jnp.max(scores, axis=-1, keepdims=True))
            weights = exponent / jnp.sum(exponent, axis=-1, keepdims=True)
            mixed = jnp.dot(
                weights.astype(jnp.bfloat16), values[rows, lanes],
                preferred_element_type=jnp.float32,
            )
            mixed_ref[tokens, lanes] = mixed.astype(jnp.bfloat16)


def attend(queries, feats, kv_weight):
    return pl.pallas_call(
        attend_kernel,
        in_specs=[IN_VMEM, IN_VMEM, IN_VMEM],
        out_shape=like(queries),
        compiler_params=PARAMS,
        name="attend",
    )(queries, feats, kv_weight)


def pick_kernel(served_ref, feats_ref, piece_ref, chosen_ref, piece_out_ref, rows_ref):
    shards_here, _, rows = feats_ref.shape
    for z in range(shards_here):
        rows_ref[z * rows : (z + 1) * rows] = feats_ref[z].T
    for peer in range(chosen_ref.shape[0]):
        for z in range(shards_here):
            start = pl.multiple_of(served_ref[peer, 0, z] * ROWBLK, ROWBLK)
            chosen_ref[peer, z] = rows_ref[pl.ds(z * rows + start, ROWBLK)]
    piece_out_ref[...] = piece_ref[...]


def pick(served, feats, piece):
    shards_here, features, rows = feats.shape
    chosen = (served.shape[0], shards_here, ROWBLK, features)
    return pl.pallas_call(
        pick_kernel,
        in_specs=[IN_SMEM, IN_VMEM, IN_VMEM],
        out_shape=(jax.ShapeDtypeStruct(chosen, feats.dtype), like(piece)),
        scratch_shapes=[pltpu.VMEM((shards_here * rows, features), feats.dtype)],
        compiler_params=PARAMS,
        name="pick",
    )(served, feats, piece)


def take_kernel(slot_ref, arrived_ref, feats_ref, rows_ref):
    spans, per_span = slot_ref.shape
    for span in range(spans):
        for at in range(per_span):
            to = (span * per_span + at) * ROWBLK
            rows_ref[to : to + ROWBLK] = arrived_ref[slot_ref[span, at]]
    feats_ref[...] = rows_ref[...].T


def take(slots, arrived):
    rows, features = slots.size * ROWBLK, arrived.shape[2]
    return pl.pallas_call(
        take_kernel,
        in_specs=[IN_SMEM, IN_VMEM],
        out_shape=jax.ShapeDtypeStruct((features, rows), arrived.dtype),
        scratch_shapes=[pltpu.VMEM((rows, features), arrived.dtype)],
        compiler_params=PARAMS,
        name="take",
    )(slots, arrived)


def project_kernel(mixed_ref, far_ref, out_ref, w_ref, sems):
    parts, groups, cols, _ = w_ref.shape
    copies = [
        pltpu.make_async_copy(
            far_ref.at[:, pl.ds(part * cols, cols)], w_ref.at[part], sems.at[part]
        )
        for part in range(parts)
    ]
    for copy in copies:
        copy.start()
    step = 256
    for part in range(parts):
        copies[part].wait()
        for col in range(0, cols, step):
            total = None
            for group in range(groups):
                partial = lax.dot_general(
                    mixed_ref[group], w_ref[part, group, col : col + step], LAST_DIMS,
                    preferred_element_type=jnp.float32,
                )
                partial = partial.astype(jnp.bfloat16).astype(jnp.float32)
                total = partial if total is None else total + partial
            to = part * cols + col
            out_ref[:, to : to + step] = total.astype(jnp.bfloat16)


def project(mixed, w_cols):
    groups, cols, width = w_cols.shape
    return pl.pallas_call(
        project_kernel,
        in_specs=[IN_VMEM, IN_HBM],
        out_shape=jax.ShapeDtypeStruct((mixed.shape[1], cols), jnp.bfloat16),
        scratch_shapes=[
            pltpu.VMEM((W_PARTS, groups, cols // W_PARTS, width), w_cols.dtype),
            pltpu.SemaphoreType.DMA((W_PARTS,)),
        ],
        compiler_params=PARAMS,
        name="project",
    )(mixed, pltpu.with_memory_space_constraint(w_cols, pltpu.HBM))


def device_index(y, z, x, c, t):
    return (((y * NZ + z) * NX + x) * NC + c) * NT + t


def to_column_owner():
    pairs = []
    for y in range(NY):
        for block in range(NZ * NX * NC):
            z, x, c = block // (NX * NC), block // NC % NX, block % NC
            new_x, new_c, new_z = block // (NC * NZ), block // NZ % NC, block % NZ
            for t in range(NT):
                target = device_index(t, new_z, new_x, new_c, y)
                pairs.append((device_index(y, z, x, c, t), target))
    return pairs


def shards(queries, encodings, kv_weight, w_out, nbr_map):
    enc_blocks = encodings.shape[0] // ROWBLK
    enc_z = lax.all_gather(encodings.T, "z", axis=0, tiled=False)
    served = lax.all_to_all(
        want(nbr_map, enc_blocks), PEERS, split_axis=0, concat_axis=0, tiled=True
    )

    piece = lax.ppermute(w_out.T, DP + ("t",), to_column_owner())

    chosen, piece = pick(served, enc_z, piece)
    arrived = lax.all_to_all(chosen, PEERS, split_axis=0, concat_axis=0, tiled=True)
    four = lax.all_gather(piece, "z", axis=0, tiled=True)
    pieces = jnp.broadcast_to(four[None], (NY * NX * NC,) + four.shape)

    slots = slot_of(nbr_map // enc_blocks)
    slots, pieces = lax.optimization_barrier((slots, pieces))
    gathered = take(slots, arrived.reshape(-1, ROWBLK, encodings.shape[1]))
    gathered, pieces = lax.optimization_barrier((gathered, pieces))
    w_cols = lax.all_to_all(pieces, PEERS, split_axis=0, concat_axis=0, tiled=True)
    w_cols = w_cols.reshape(NY, -1, w_cols.shape[2])
    feats = lax.all_gather(gathered, "t", axis=0, tiled=True)

    mixed = attend(queries, feats, kv_weight)
    mixed = lax.all_gather(mixed, "t", axis=0, tiled=False)
    return project(mixed, w_cols)


def solution(mesh):
    fine = Mesh(mesh.devices.reshape(NY, NZ, NX, NC, NT), DP + ("t",))
    return jax.shard_map(
        shards,
        mesh=fine,
        in_specs=(
            P(DP, "t"),
            P(DP, "t"),
            P(None, None, "t"),
            P("t", DP),
            P(DP, None),
        ),
        out_specs=P(DP, "t"),
        check_vma=False,
    )
```

time: 188 us -> 147 us (0.78)
  waiting for transfers between devices: 41.1 us -> 3.42 us
  between operations: 13.5 us -> 0.1 us
  blocking collectives: 82.4 us -> 95.1 us
  local copies, waits for them, and re-layouts: 7.17 us -> 2.44 us
  Pallas kernels: 7.56 us -> 10.4 us
    all_to_all x2 -> x3, waiting for transfers between devices: 38.2 us -> 3.42 us  [the longest x1 3.41 us: shards(): lax.all_to_all(chosen, PEERS, split_axis=0, concat_axis=0, tiled=True)]
    all_gather x1 -> x2, blocking collectives: 17 us -> 34.9 us  [the longest x1 23.6 us: shards(): enc_z = lax.all_gather(encodings.T, 'z', axis=0, tiled=False)]
    all_to_all x2 -> x3, starting transfers between devices: 28 us -> 31.7 us  [the longest x1 15.1 us: shards(): lax.all_to_all(chosen, PEERS, split_axis=0, concat_axis=0, tiled=True)]
    all_gather x1, blocking collectives: 41.3 us -> 37.6 us  [shards(): feats = lax.all_gather(gathered, 't', axis=0, tiled=True)]
    unnamed x9 -> x6, local copies, waits for them, and re-layouts: 3.27 us -> 0.02 us
    ppermute x1, starting transfers between devices: 5.06 us -> 1.92 us  [shards(): piece = lax.ppermute(w_out.T, DP + ('t',), to_column_owner())]
    ppermute x1, waiting for transfers between devices: 2.9 us -> 0.01 us  [shards(): piece = lax.ppermute(w_out.T, DP + ('t',), to_column_owner())]
    pallas_call x2 -> x4, Pallas kernels: 7.56 us -> 10.4 us  [the longest x1 3.94 us: project(): pl.pallas_call(project_kernel, in_specs=[IN_VMEM, IN_HBM], out_shape=jax....]
  transfers between devices with their start and end apart: 4 -> 4, of which waited for: 3 -> 1; matrix products, arithmetic and copies ran while one was open for 4% -> 2% of each run, Pallas kernels for 2% -> 2%
where the time goes in v4:
time: 147 us
  blocking collectives  95.1 us (65%)
  starting transfers between devices  33.6 us (23%)
  Pallas kernels  10.4 us (7%)
  waiting for transfers between devices  3.42 us (2%)
  local copies, waits for them, and re-layouts  2.44 us (2%)
  other arithmetic  1.59 us (1%)
    all_gather x1, blocking collectives, shards(): feats = lax.all_gather(gathered, 't', axis=0, tiled=True)  37.6 us
    all_gather x1, blocking collectives, shards(): enc_z = lax.all_gather(encodings.T, 'z', axis=0, tiled=False)  23.6 us
    all_gather x1, blocking collectives, shards(): mixed = lax.all_gather(mixed, 't', axis=0, tiled=False)  22.6 us
    all_to_all x1, starting transfers between devices, shards(): lax.all_to_all(chosen, PEERS, split_axis=0, concat_axis=0, tiled=True)  15.1 us
    all_gather x1, blocking collectives, shards(): four = lax.all_gather(piece, 'z', axis=0, tiled=True)  11.3 us
    all_to_all x1, starting transfers between devices, shards(): lax.all_to_all(want(nbr_map, enc_blocks), PEERS, split_axis=0, concat_axi...  10.4 us
    all_to_all x1, starting transfers between devices, shards(): lax.all_to_all(pieces, PEERS, split_axis=0, concat_axis=0, tiled=True)  6.22 us
    pallas_call x1, Pallas kernels, project(): pl.pallas_call(project_kernel, in_specs=[IN_VMEM, IN_HBM], out_shape=jax....  3.94 us
  transfers between devices with their start and end apart: 4, of which 1 were waited for; matrix products, arithmetic and copies ran while one was open for 2% of the time, Pallas kernels for 2%

profile of v4, /device:TPU:1, one launch (start us, length us, event | category | flops | bytes accessed | tf_op | source)
XLA Modules:
  0.0 146.7 jit_solution(18344744421182529576)
XLA Ops:
  0.0 0.7 and_add_fusion
  0.8 0.1 add_select_fusion
  0.8 0.1 select_reduce_fusion
  1.0 0.6 convert_element_type.31
  1.6 10.4 %all-to-all-start = ((s32[32,1,128]{2,1,0:T(1,128)}), s32[32,1,128]{2,1,0:T(1,128)S(1)}, u32[]{:S(2)}, u32[]{:S(2)}) async-start(s32[32,1,128]{2,1,0:T(1,128)} %bitcast), calls=%async_computation | async-start | bytes 32768 | tf_op jit(solution)/shard_map/all_to_all | solution.py:189
  12.0 1.9 %collective-permute-start = (bf16[32,512]{1,0:T(8,128)(2,1)}, bf16[32,512]{1,0:T(8,128)(2,1)S(1)}, u32[]{:S(2)}, u32[]{:S(2)}) collective-permute-start(bf16[32,512]{1,0:T(8,128)(2,1)} %bitcast.11), channel_id=1, source_target_pairs={{0,0},{1,128},{2,256},{3,384},{4,32},{5,160},{6,288},{7,416},{8,64... | collective-permute-start | bytes 98312 | tf_op jit(solution)/shard_map/ppermute | solution.py:193
  13.9 23.6 %all-gather = bf16[896,512]{1,0:T(8,128)(2,1)S(1)} all-gather(bf16[224,512]{1,0:T(8,128)(2,1)} %bitcast.10), channel_id=2, replica_groups=mesh['y'=4,'z'=4,'x'=4,'c'=2,'t'=4] {'z'}, dimensions={0}, use_global_device_ids=true | all-gather | bytes 1146880 | tf_op jit(solution)/shard_map/all_gather | solution.py:188
  37.5 0.0 all-to-all-done.served_ref
  37.5 0.0 collective-permute-done.piece_ref
  37.5 2.2 %pick.1 = (bf16[32,4,16,224]{3,2,1,0:T(8,128)(2,1)}, bf16[32,512]{1,0:T(8,128)(2,1)S(1)}) custom-call(s32[32,1,128]{2,1,0:T(1,128)S(1)} %all-to-all-done.served_ref, bf16[4,224,512]{2,1,0:T(8,128)(2,1)S(1)} %bitcast.8, bf16[32,512]{1,0:T(8,128)(2,1)S(1)} %collective-permute-done.piece_ref), custom_call_target="tpu_custom_call" | custom-call | tf_op jit(solution)/shard_map/pick/pallas_call | solution.py:98
  39.7 15.1 %all-to-all-start.1 = ((bf16[32,4,16,224]{3,2,1,0:T(8,128)(2,1)}), bf16[32,4,16,224]{3,2,1,0:T(8,128)(2,1)S(1)}, u32[]{:S(2)}, u32[]{:S(2)}) async-start(bf16[32,4,16,224]{3,2,1,0:T(8,128)(2,1)} %get-tuple-element.16), calls=%async_computation.1 | async-start | bytes 2097152 | tf_op jit(solution)/shard_map/all_to_all | solution.py:196
  54.8 11.3 %all_gather.20 = bf16[128,512]{1,0:T(8,128)(2,1)S(1)} all-gather(bf16[32,512]{1,0:T(8,128)(2,1)S(1)} %get-tuple-element.14), channel_id=1, replica_groups=mesh['y'=4,'z'=4,'x'=4,'c'=2,'t'=4] {'z'}, dimensions={0}, use_global_device_ids=true | all-gather | bytes 163840 | tf_op jit(solution)/shard_map/all_gather | solution.py:197
  66.1 2.4 %broadcast_in_dim.40 = bf16[32,128,512]{2,1,0:T(8,128)(2,1)} broadcast(bf16[128,512]{1,0:T(8,128)(2,1)S(1)} %all_gather.20), dimensions={1,2} | broadcast | bytes 4325376 | tf_op jit(solution)/shard_map/broadcast_in_dim | solution.py:198
  68.6 3.4 %all-to-all-done.1 = bf16[32,4,16,224]{3,2,1,0:T(8,128)(2,1)S(1)} async-done(((bf16[32,4,16,224]{3,2,1,0:T(8,128)(2,1)}), bf16[32,4,16,224]{3,2,1,0:T(8,128)(2,1)S(1)}, u32[]{:S(2)}, u32[]{:S(2)}) %all-to-all-start.1) | async-done | bytes 917536 | tf_op jit(solution)/shard_map/all_to_all | solution.py:196
  72.0 0.7 take.1
  72.7 0.0 copy-start
  72.7 0.0 copy-start.1
  72.7 6.2 %all-to-all-start.2 = ((bf16[32,128,512]{2,1,0:T(8,128)(2,1)}), bf16[32,128,512]{2,1,0:T(8,128)(2,1)}, u32[]{:S(2)}, u32[]{:S(2)}) async-start(bf16[32,128,512]{2,1,0:T(8,128)(2,1)} %broadcast_in_dim.40), calls=%async_computation.2 | async-start | bytes 8388608 | tf_op jit(solution)/shard_map/all_to_all | solution.py:204
  78.9 37.6 %all_gather.21.feat_ref = bf16[896,512]{1,0:T(8,128)(2,1)S(1)} all-gather(bf16[224,512]{1,0:T(8,128)(2,1)S(1)} %take.1), channel_id=1, replica_groups=mesh['y'=4,'z'=4,'x'=4,'c'=2,'t'=4] {'t'}, dimensions={0}, use_global_device_ids=true | all-gather | bytes 1146880 | tf_op jit(solution)/shard_map/all_gather | solution.py:206
  116.6 0.0 copy-done
  116.6 3.6 %attend.1 = bf16[128,512]{1,0:T(8,128)(2,1)S(1)} custom-call(bf16[128,512]{1,0:T(8,128)(2,1)S(1)} %copy-done.1, bf16[896,512]{1,0:T(8,128)(2,1)S(1)} %all_gather.21.feat_ref, bf16[2,896,512]{2,1,0:T(8,128)(2,1)S(1)} %copy-done), custom_call_target="tpu_custom_call" | custom-call | tf_op jit(solution)/shard_map/attend/pallas_call | solution.py:75
  120.1 22.6 %all-gather.1 = bf16[512,512]{1,0:T(8,128)(2,1)S(1)} all-gather(bf16[128,512]{1,0:T(8,128)(2,1)S(1)} %attend.1), channel_id=3, replica_groups=mesh['y'=4,'z'=4,'x'=4,'c'=2,'t'=4] {'t'}, dimensions={0}, use_global_device_ids=true | all-gather | bytes 655360 | tf_op jit(solution)/shard_map/all_gather | solution.py:209
  142.7 0.0 all-to-all-done.2
  142.7 3.9 %project.1 = bf16[128,1024]{1,0:T(8,128)(2,1)} custom-call(bf16[4,128,512]{2,1,0:T(8,128)(2,1)S(1)} %bitcast.9, bf16[4,1024,512]{2,1,0:T(8,128)(2,1)} %bitcast.6.far_ref), custom_call_target="tpu_custom_call" | custom-call | tf_op jit(solution)/shard_map/project/pallas_call | solution.py:157
  (6 shorter events, 0.0 us)
Async XLA Ops:
  0.0 54.8 %copy-start.2 = (s32[2,16]{1,0:T(2,128)S(1)}, s32[2,16]{1,0:T(2,128)}, u32[]{:S(2)}) copy-start(s32[2,16]{1,0:T(2,128)} %param.15) | copy-start | bytes 388
  1.6 35.9 %all-to-all-start = ((s32[32,1,128]{2,1,0:T(1,128)}), s32[32,1,128]{2,1,0:T(1,128)S(1)}, u32[]{:S(2)}, u32[]{:S(2)}) async-start(s32[32,1,128]{2,1,0:T(1,128)} %bitcast), calls=%async_computation | async-start | bytes 32768 | tf_op jit(solution)/shard_map/all_to_all | solution.py:189
  12.0 25.5 %collective-permute-start = (bf16[32,512]{1,0:T(8,128)(2,1)}, bf16[32,512]{1,0:T(8,128)(2,1)S(1)}, u32[]{:S(2)}, u32[]{:S(2)}) collective-permute-start(bf16[32,512]{1,0:T(8,128)(2,1)} %bitcast.11), channel_id=1, source_target_pairs={{0,0},{1,128},{2,256},{3,384},{4,32},{5,160},{6,288},{7,416},{8,64... | collective-permute-start | bytes 98312 | tf_op jit(solution)/shard_map/ppermute | solution.py:193
  39.7 32.3 %all-to-all-start.1 = ((bf16[32,4,16,224]{3,2,1,0:T(8,128)(2,1)}), bf16[32,4,16,224]{3,2,1,0:T(8,128)(2,1)S(1)}, u32[]{:S(2)}, u32[]{:S(2)}) async-start(bf16[32,4,16,224]{3,2,1,0:T(8,128)(2,1)} %get-tuple-element.16), calls=%async_computation.1 | async-start | bytes 2097152 | tf_op jit(solution)/shard_map/all_to_all | solution.py:196
  72.7 43.9 %copy-start = (bf16[2,896,512]{2,1,0:T(8,128)(2,1)S(1)}, bf16[2,896,512]{2,1,0:T(8,128)(2,1)}, u32[]{:S(2)}) copy-start(bf16[2,896,512]{2,1,0:T(8,128)(2,1)} %kv_ref.1) | copy-start | bytes 5505028
  72.7 43.9 %copy-start.1 = (bf16[128,512]{1,0:T(8,128)(2,1)S(1)}, bf16[128,512]{1,0:T(8,128)(2,1)}, u32[]{:S(2)}) copy-start(bf16[128,512]{1,0:T(8,128)(2,1)} %q_ref.1) | copy-start | bytes 393220
  72.7 70.0 %all-to-all-start.2 = ((bf16[32,128,512]{2,1,0:T(8,128)(2,1)}), bf16[32,128,512]{2,1,0:T(8,128)(2,1)}, u32[]{:S(2)}, u32[]{:S(2)}) async-start(bf16[32,128,512]{2,1,0:T(8,128)(2,1)} %broadcast_in_dim.40), calls=%async_computation.2 | async-start | bytes 8388608 | tf_op jit(solution)/shard_map/all_to_all | solution.py:204

commit v5 on v4

--- a/solution.py
+++ b/solution.py
@@ -12,7 +12,6 @@
 SPAN = 64
 ROWBLK = 16
 LANES = 128
-W_PARTS = 2
 NY, NZ, NX, NC, NT = 4, 4, 4, 2, 4
 DP = ("y", "z", "x", "c")
 PEERS = ("y", "x", "c")
@@ -35,13 +34,13 @@
 
 
 def want(nbr_map, enc_blocks):
-    blocks = nbr_map.astype(jnp.uint32)
-    lane = jnp.arange(LANES, dtype=jnp.uint32)[None, :]
-    code = jnp.arange(NY * NX * NC, dtype=jnp.uint32)[:, None] * NZ + lane
-    code = jnp.where(lane < NZ, code, NY * NX * NC * NZ)
-    here = slot_of(blocks // enc_blocks)[:, :, None, None] == code
-    wanted = jnp.where(here, (blocks % enc_blocks)[:, :, None, None], 0)
-    return jnp.sum(wanted, axis=(0, 1)).astype(jnp.int32)[:, None, :]
+    z = jnp.arange(LANES, dtype=jnp.int32)[None, :]
+    peer = jnp.arange(NY * NX * NC, dtype=jnp.int32)[:, None]
+    shard = (peer // (NX * NC) * NZ + z) * (NX * NC) + peer % (NX * NC)
+    shard = jnp.where(z < NZ, shard, NY * NZ * NX * NC)
+    row_block = nbr_map[:, :, None, None] - shard * enc_blocks
+    wanted = jnp.where((row_block >= 0) & (row_block < enc_blocks), row_block, 0)
+    return jnp.sum(wanted, axis=(0, 1))[:, None, :]
 
 
 def attend_kernel(q_ref, feat_ref, kv_ref, mixed_ref):
@@ -81,28 +80,29 @@
     )(queries, feats, kv_weight)
 
 
-def pick_kernel(served_ref, feats_ref, piece_ref, chosen_ref, piece_out_ref, rows_ref):
-    shards_here, _, rows = feats_ref.shape
-    for z in range(shards_here):
-        rows_ref[z * rows : (z + 1) * rows] = feats_ref[z].T
+def pick_kernel(z_ref, served_ref, *refs):
+    held_refs, (chosen_ref, rows_ref) = refs[:NZ], refs[NZ:]
+    features, rows = chosen_ref.shape[-1], held_refs[0].shape[1]
+    for bits, held_ref in enumerate(held_refs):
+        rows_ref[bits * rows : (bits + 1) * rows] = held_ref[:features].T
+    base = [(z_ref[0] ^ z) * rows for z in range(NZ)]
     for peer in range(chosen_ref.shape[0]):
-        for z in range(shards_here):
-            start = pl.multiple_of(served_ref[peer, 0, z] * ROWBLK, ROWBLK)
-            chosen_ref[peer, z] = rows_ref[pl.ds(z * rows + start, ROWBLK)]
-    piece_out_ref[...] = piece_ref[...]
-
-
-def pick(served, feats, piece):
-    shards_here, features, rows = feats.shape
-    chosen = (served.shape[0], shards_here, ROWBLK, features)
+        for z in range(NZ):
+            start = pl.multiple_of(base[z] + served_ref[peer, 0, z] * ROWBLK, ROWBLK)
+            chosen_ref[peer, z] = rows_ref[pl.ds(start, ROWBLK)]
+
+
+def pick(my_z, served, held):
+    features, rows = held[0].shape
+    chosen = (served.shape[0], NZ, ROWBLK, features)
     return pl.pallas_call(
         pick_kernel,
-        in_specs=[IN_SMEM, IN_VMEM, IN_VMEM],
-        out_shape=(jax.ShapeDtypeStruct(chosen, feats.dtype), like(piece)),
-        scratch_shapes=[pltpu.VMEM((shards_here * rows, features), feats.dtype)],
+        in_specs=[IN_SMEM, IN_SMEM] + [IN_VMEM] * NZ,
+        out_shape=jax.ShapeDtypeStruct(chosen, held[0].dtype),
+        scratch_shapes=[pltpu.VMEM((NZ * rows, features), held[0].dtype)],
         compiler_params=PARAMS,
         name="pick",
-    )(served, feats, piece)
+    )(my_z, served, *held)
 
 
 def take_kernel(slot_ref, arrived_ref, feats_ref, rows_ref):
@@ -126,41 +126,42 @@
     )(slots, arrived)
 
 
-def project_kernel(mixed_ref, far_ref, out_ref, w_ref, sems):
-    parts, groups, cols, _ = w_ref.shape
+def project_kernel(mixed_ref, far_ref, out_ref, w_ref, total_ref, sems):
+    groups, cols, _ = w_ref.shape
     copies = [
-        pltpu.make_async_copy(
-            far_ref.at[:, pl.ds(part * cols, cols)], w_ref.at[part], sems.at[part]
-        )
-        for part in range(parts)
+        pltpu.make_async_copy(far_ref.at[group], w_ref.at[group], sems.at[group])
+        for group in range(groups)
     ]
     for copy in copies:
         copy.start()
     step = 256
-    for part in range(parts):
-        copies[part].wait()
+    for group in range(groups):
+        copies[group].wait()
         for col in range(0, cols, step):
-            total = None
-            for group in range(groups):
-                partial = lax.dot_general(
-                    mixed_ref[group], w_ref[part, group, col : col + step], LAST_DIMS,
-                    preferred_element_type=jnp.float32,
-                )
-                partial = partial.astype(jnp.bfloat16).astype(jnp.float32)
-                total = partial if total is None else total + partial
-            to = part * cols + col
-            out_ref[:, to : to + step] = total.astype(jnp.bfloat16)
+            here = slice(col, col + step)
+            partial = lax.dot_general(
+                mixed_ref[group], w_ref[group, here], LAST_DIMS,
+                preferred_element_type=jnp.float32,
+            )
+            partial = partial.astype(jnp.bfloat16).astype(jnp.float32)
+            total = partial if group == 0 else total_ref[:, here] + partial
+            if group == groups - 1:
+                out_ref[:, here] = total.astype(jnp.bfloat16)
+            else:
+                total_ref[:, here] = total
 
 
 def project(mixed, w_cols):
-    groups, cols, width = w_cols.shape
+    groups, cols, _ = w_cols.shape
+    tokens = mixed.shape[1]
     return pl.pallas_call(
         project_kernel,
         in_specs=[IN_VMEM, IN_HBM],
-        out_shape=jax.ShapeDtypeStruct((mixed.shape[1], cols), jnp.bfloat16),
+        out_shape=jax.ShapeDtypeStruct((tokens, cols), jnp.bfloat16),
         scratch_shapes=[
-            pltpu.VMEM((W_PARTS, groups, cols // W_PARTS, width), w_cols.dtype),
-            pltpu.SemaphoreType.DMA((W_PARTS,)),
+            pltpu.VMEM(w_cols.shape, w_cols.dtype),
+            pltpu.VMEM((tokens, cols), jnp.float32),
+            pltpu.SemaphoreType.DMA((groups,)),
         ],
         compiler_params=PARAMS,
         name="project",
@@ -176,32 +177,41 @@
     for y in range(NY):
         for block in range(NZ * NX * NC):
             z, x, c = block // (NX * NC), block // NC % NX, block % NC
-            new_x, new_c, new_z = block // (NC * NZ), block // NZ % NC, block % NZ
+            new_x, new_z, new_c = block // (NZ * NC), block // NC % NZ, block % NC
             for t in range(NT):
                 target = device_index(t, new_z, new_x, new_c, y)
                 pairs.append((device_index(y, z, x, c, t), target))
     return pairs
 
 
+def from_z(value, bits):
+    return lax.ppermute(value, "z", [(z, z ^ bits) for z in range(NZ)])
+
+
 def shards(queries, encodings, kv_weight, w_out, nbr_map):
     enc_blocks = encodings.shape[0] // ROWBLK
-    enc_z = lax.all_gather(encodings.T, "z", axis=0, tiled=False)
-    served = lax.all_to_all(
-        want(nbr_map, enc_blocks), PEERS, split_axis=0, concat_axis=0, tiled=True
-    )
-
-    piece = lax.ppermute(w_out.T, DP + ("t",), to_column_owner())
-
-    chosen, piece = pick(served, enc_z, piece)
+    features = encodings.shape[1]
+    my_z = lax.axis_index("z").astype(jnp.int32).reshape(1)
+    wanted = want(nbr_map, enc_blocks)
+    piece, wanted = lax.optimization_barrier((w_out.T, wanted))
+    piece = lax.ppermute(piece, DP + ("t",), to_column_owner())
+
+    feats = encodings.T
+    served = lax.all_to_all(wanted, PEERS, split_axis=0, concat_axis=0, tiled=True)
+    one, two = from_z(feats, 1), from_z(feats, 2)
+    two, served, piece = lax.optimization_barrier((two, served, piece))
+    chosen = pick(my_z, served, [feats, one, two, from_z(two, 1)])
     arrived = lax.all_to_all(chosen, PEERS, split_axis=0, concat_axis=0, tiled=True)
-    four = lax.all_gather(piece, "z", axis=0, tiled=True)
-    pieces = jnp.broadcast_to(four[None], (NY * NX * NC,) + four.shape)
+
+    chosen, piece = lax.optimization_barrier((chosen, piece))
+    four = lax.all_gather(piece, ("z", "c"), axis=0, tiled=True)
+    pieces = jnp.broadcast_to(four[None], (NY * NX,) + four.shape)
 
     slots = slot_of(nbr_map // enc_blocks)
     slots, pieces = lax.optimization_barrier((slots, pieces))
-    gathered = take(slots, arrived.reshape(-1, ROWBLK, encodings.shape[1]))
+    gathered = take(slots, arrived.reshape(-1, ROWBLK, features))
     gathered, pieces = lax.optimization_barrier((gathered, pieces))
-    w_cols = lax.all_to_all(pieces, PEERS, split_axis=0, concat_axis=0, tiled=True)
+    w_cols = lax.all_to_all(pieces, ("y", "x"), split_axis=0, concat_axis=0, tiled=True)
     w_cols = w_cols.reshape(NY, -1, w_cols.shape[2])
     feats = lax.all_gather(gathered, "t", axis=0, tiled=True)
 

time: 147 us -> 147 us (level)
  blocking collectives: 95.1 us -> 68.4 us
  starting transfers between devices: 33.6 us -> 46.9 us
  waiting for transfers between devices: 3.42 us -> 14.1 us
    all_gather x2 -> x1, blocking collectives: 34.9 us -> 14.4 us  [shards(): four = lax.all_gather(piece, ('z', 'c'), axis=0, tiled=True)]
    ppermute x1 -> x4, starting transfers between devices: 1.92 us -> 13.7 us  [the longest x3 12.3 us: from_z(): return lax.ppermute(value, 'z', [(z, z ^ bits) for z in range(NZ)])]
    all_to_all x2, starting transfers between devices: 16.6 us -> 26.4 us  [the longest x1 19.4 us: shards(): lax.all_to_all(wanted, PEERS, split_axis=0, concat_axis=0, tiled=True)]
    all_to_all x2, waiting for transfers between devices: 0.01 us -> 9.02 us  [the longest x1 5.45 us: shards(): lax.all_to_all(pieces, ('y', 'x'), split_axis=0, concat_axis=0, tiled=True)]
    all_to_all x1, starting transfers between devices: 15.1 us -> 6.81 us  [shards(): lax.all_to_all(chosen, PEERS, split_axis=0, concat_axis=0, tiled=True)]
    ppermute x1 -> x4, waiting for transfers between devices: 0.01 us -> 5.1 us  [the longest x3 5.1 us: from_z(): return lax.ppermute(value, 'z', [(z, z ^ bits) for z in range(NZ)])]
    all_gather x1, blocking collectives: 37.6 us -> 33.4 us  [shards(): feats = lax.all_gather(gathered, 't', axis=0, tiled=True)]
    all_to_all x1, waiting for transfers between devices: 3.41 us -> 0.01 us  [shards(): lax.all_to_all(chosen, PEERS, split_axis=0, concat_axis=0, tiled=True)]
  transfers between devices with their start and end apart: 4 -> 7, of which waited for: 1 -> 3; matrix products, arithmetic and copies ran while one was open for 2% -> 3% of each run, Pallas kernels for 2% -> 2%
where the time goes in v5:
time: 147 us; the launch traced here: 145 us
  blocking collectives  68.4 us (47%)
  starting transfers between devices  46.9 us (32%)
  waiting for transfers between devices  14.1 us (10%)
  Pallas kernels  10.4 us (7%)
  local copies, waits for them, and re-layouts  3.31 us (2%)
  other arithmetic  2.25 us (2%)
    all_gather x1, blocking collectives, shards(): feats = lax.all_gather(gathered, 't', axis=0, tiled=True)  33.4 us
    all_gather x1, blocking collectives, shards(): mixed = lax.all_gather(mixed, 't', axis=0, tiled=False)  20.7 us
    all_to_all x1, starting transfers between devices, shards(): lax.all_to_all(wanted, PEERS, split_axis=0, concat_axis=0, tiled=True)  19.4 us
    all_gather x1, blocking collectives, shards(): four = lax.all_gather(piece, ('z', 'c'), axis=0, tiled=True)  14.4 us
    ppermute x3, starting transfers between devices, from_z(): return lax.ppermute(value, 'z', [(z, z ^ bits) for z in range(NZ)])  12.3 us
    all_to_all x1, starting transfers between devices, shards(): lax.all_to_all(pieces, ('y', 'x'), split_axis=0, concat_axis=0, tiled=True)  7.01 us
    all_to_all x1, starting transfers between devices, shards(): lax.all_to_all(chosen, PEERS, split_axis=0, concat_axis=0, tiled=True)  6.81 us
    all_to_all x1, waiting for transfers between devices, shards(): lax.all_to_all(pieces, ('y', 'x'), split_axis=0, concat_axis=0, tiled=True)  5.45 us
  transfers between devices with their start and end apart: 7, of which 3 were waited for; matrix products, arithmetic and copies ran while one was open for 3% of the time, Pallas kernels for 2%

profile of v5, /device:TPU:1, one launch (start us, length us, event | category | flops | bytes accessed | tf_op | source)
XLA Modules:
  0.0 145.4 jit_solution(7716660435332610301)
XLA Ops:
  0.0 5.7 %collective-permute-start = (bf16[224,512]{1,0:T(8,128)(2,1)}, bf16[224,512]{1,0:T(8,128)(2,1)S(1)}, u32[]{:S(2)}, u32[]{:S(2)}) collective-permute-start(bf16[224,512]{1,0:T(8,128)(2,1)} %bitcast.9), channel_id=1, source_target_pairs={{0,64},{32,96},{64,0},{96,32},{1,65},{33,97},{65,1},{97,33},{2,66}... | collective-permute-start | bytes 688136 | tf_op jit(solution)/shard_map/ppermute | solution.py:188
  5.8 0.1 select_multiply_fusion
  5.8 1.5 %fusion = s32[32,128]{1,0:T(8,128)} fusion(s32[32,128]{1,0:T(8,128)S(1)} %select_multiply_fusion, s32[2,16]{1,0:T(2,128)} %param.9), kind=kLoop, calls=%fused_computation.3 | loop fusion | flops 782336 | bytes 32896 | tf_op jit(solution)/shard_map/reduce_sum | solution.py:43
  7.3 1.4 collective-permute-start.1
  8.7 19.4 %all-to-all-start = ((s32[32,1,128]{2,1,0:T(1,128)}), s32[32,1,128]{2,1,0:T(1,128)S(1)}, u32[]{:S(2)}, u32[]{:S(2)}) async-start(s32[32,1,128]{2,1,0:T(1,128)} %bitcast.3), calls=%async_computation | async-start | bytes 32768 | tf_op jit(solution)/shard_map/all_to_all | solution.py:200
  28.1 3.3 %collective-permute-start.2 = (bf16[224,512]{1,0:T(8,128)(2,1)}, bf16[224,512]{1,0:T(8,128)(2,1)S(1)}, u32[]{:S(2)}, u32[]{:S(2)}) collective-permute-start(bf16[224,512]{1,0:T(8,128)(2,1)} %bitcast.10), channel_id=1, source_target_pairs={{0,32},{32,0},{64,96},{96,64},{1,33},{33,1},{65,97},{97,65},{2,34}... | collective-permute-start | bytes 688136 | tf_op jit(solution)/shard_map/ppermute | solution.py:188
  31.4 3.6 %all-to-all-done.served_ref = s32[32,1,128]{2,1,0:T(1,128)S(1)} async-done(((s32[32,1,128]{2,1,0:T(1,128)}), s32[32,1,128]{2,1,0:T(1,128)S(1)}, u32[]{:S(2)}, u32[]{:S(2)}) %all-to-all-start) | async-done | bytes 16416 | tf_op jit(solution)/shard_map/all_to_all | solution.py:200
  34.9 3.3 %collective-permute-start.3 = (bf16[224,512]{1,0:T(8,128)(2,1)S(1)}, bf16[224,512]{1,0:T(8,128)(2,1)S(1)}, u32[]{:S(2)}, u32[]{:S(2)}) collective-permute-start(bf16[224,512]{1,0:T(8,128)(2,1)S(1)} %collective-permute-done.refs_2_), channel_id=1, source_target_pairs={{0,32},{32,0},{64,96},{96,64},{1,33},{33,1},{65,97},{97,65},{2,34}... | collective-permute-start | bytes 688136 | tf_op jit(solution)/shard_map/ppermute | solution.py:188
  38.2 5.1 %collective-permute-done.3.refs_3_ = bf16[224,512]{1,0:T(8,128)(2,1)S(1)} collective-permute-done((bf16[224,512]{1,0:T(8,128)(2,1)S(1)}, bf16[224,512]{1,0:T(8,128)(2,1)S(1)}, u32[]{:S(2)}, u32[]{:S(2)}) %collective-permute-start.3) | collective-permute-done | bytes 229408 | tf_op jit(solution)/shard_map/ppermute | solution.py:188
  43.3 0.9 copy-done.1
  44.3 2.3 %pick.1 = bf16[32,4,16,224]{3,2,1,0:T(8,128)(2,1)} custom-call(s32[1]{0:T(128)} %bitcast.z_ref, s32[32,1,128]{2,1,0:T(1,128)S(1)} %all-to-all-done.served_ref, bf16[224,512]{1,0:T(8,128)(2,1)S(1)} %bitcast.11, bf16[224,512]{1,0:T(8,128)(2,1)S(1)} %collective-permute-done.2.refs_1_, bf16[224,512]{1,0:T(8,128)(2,1)S(1)} %collective-permute-done.refs_2_, ...), custom_call_target="tpu_custom_call" | custom-call | tf_op jit(solution)/shard_map/pick/pallas_call | solution.py:98
  46.5 6.8 %all-to-all-start.1 = ((bf16[32,4,16,224]{3,2,1,0:T(8,128)(2,1)}), bf16[32,4,16,224]{3,2,1,0:T(8,128)(2,1)S(1)}, u32[]{:S(2)}, u32[]{:S(2)}) async-start(bf16[32,4,16,224]{3,2,1,0:T(8,128)(2,1)} %pick.1), calls=%async_computation.1 | async-start | bytes 2097152 | tf_op jit(solution)/shard_map/all_to_all | solution.py:204
  53.3 0.7 fusion.2.slot_ref
  54.0 14.4 %all_gather.12 = bf16[256,512]{1,0:T(8,128)(2,1)S(1)} all-gather(bf16[32,512]{1,0:T(8,128)(2,1)S(1)} %collective-permute-done.1), channel_id=1, replica_groups=mesh['y'=4,'z'=4,'x'=4,'c'=2,'t'=4] {'z','c'}, dimensions={0}, use_global_device_ids=true | all-gather | bytes 294912 | tf_op jit(solution)/shard_map/all_gather | solution.py:207
  68.4 2.4 %broadcast_in_dim.30 = bf16[16,256,512]{2,1,0:T(8,128)(2,1)} broadcast(bf16[256,512]{1,0:T(8,128)(2,1)S(1)} %all_gather.12), dimensions={1,2} | broadcast | bytes 4456448 | tf_op jit(solution)/shard_map/broadcast_in_dim | solution.py:208
  70.8 0.7 take.1
  71.4 0.0 copy-start
  71.5 0.0 copy-start.2
  71.5 7.0 %all-to-all-start.2 = ((bf16[16,256,512]{2,1,0:T(8,128)(2,1)}), bf16[16,256,512]{2,1,0:T(8,128)(2,1)}, u32[]{:S(2)}, u32[]{:S(2)}) async-start(bf16[16,256,512]{2,1,0:T(8,128)(2,1)} %broadcast_in_dim.30), calls=%async_computation.2 | async-start | bytes 8388608 | tf_op jit(solution)/shard_map/all_to_all | solution.py:214
  78.5 33.4 %all_gather.13.feat_ref = bf16[896,512]{1,0:T(8,128)(2,1)S(1)} all-gather(bf16[224,512]{1,0:T(8,128)(2,1)S(1)} %take.1), channel_id=1, replica_groups=mesh['y'=4,'z'=4,'x'=4,'c'=2,'t'=4] {'t'}, dimensions={0}, use_global_device_ids=true | all-gather | bytes 1146880 | tf_op jit(solution)/shard_map/all_gather | solution.py:216
  111.8 3.6 %attend.1 = bf16[128,512]{1,0:T(8,128)(2,1)S(1)} custom-call(bf16[128,512]{1,0:T(8,128)(2,1)S(1)} %copy-done.2, bf16[896,512]{1,0:T(8,128)(2,1)S(1)} %all_gather.13.feat_ref, bf16[2,896,512]{2,1,0:T(8,128)(2,1)S(1)} %copy-done), custom_call_target="tpu_custom_call" | custom-call | tf_op jit(solution)/shard_map/attend/pallas_call | solution.py:74
  115.4 20.7 %all-gather = bf16[512,512]{1,0:T(8,128)(2,1)S(1)} all-gather(bf16[128,512]{1,0:T(8,128)(2,1)S(1)} %attend.1), channel_id=2, replica_groups=mesh['y'=4,'z'=4,'x'=4,'c'=2,'t'=4] {'t'}, dimensions={0}, use_global_device_ids=true | all-gather | bytes 655360 | tf_op jit(solution)/shard_map/all_gather | solution.py:219
  136.1 5.4 %all-to-all-done.2 = bf16[16,256,512]{2,1,0:T(8,128)(2,1)} async-done(((bf16[16,256,512]{2,1,0:T(8,128)(2,1)}), bf16[16,256,512]{2,1,0:T(8,128)(2,1)}, u32[]{:S(2)}, u32[]{:S(2)}) %all-to-all-start.2) | async-done | bytes 4194336 | tf_op jit(solution)/shard_map/all_to_all | solution.py:214
  141.5 3.9 %project.1 = bf16[128,1024]{1,0:T(8,128)(2,1)} custom-call(bf16[4,128,512]{2,1,0:T(8,128)(2,1)S(1)} %bitcast.8, bf16[4,1024,512]{2,1,0:T(8,128)(2,1)} %bitcast.6.far_ref), custom_call_target="tpu_custom_call" | custom-call | tf_op jit(solution)/shard_map/project/pallas_call | solution.py:157
  (9 shorter events, 0.0 us)
Async XLA Ops:
  0.0 34.9 %collective-permute-start = (bf16[224,512]{1,0:T(8,128)(2,1)}, bf16[224,512]{1,0:T(8,128)(2,1)S(1)}, u32[]{:S(2)}, u32[]{:S(2)}) collective-permute-start(bf16[224,512]{1,0:T(8,128)(2,1)} %bitcast.9), channel_id=1, source_target_pairs={{0,64},{32,96},{64,0},{96,32},{1,65},{33,97},{65,1},{97,33},{2,66}... | collective-permute-start | bytes 688136 | tf_op jit(solution)/shard_map/ppermute | solution.py:188
  7.3 27.7 %collective-permute-start.1 = (bf16[32,512]{1,0:T(8,128)(2,1)}, bf16[32,512]{1,0:T(8,128)(2,1)S(1)}, u32[]{:S(2)}, u32[]{:S(2)}) collective-permute-start(bf16[32,512]{1,0:T(8,128)(2,1)} %bitcast.12), channel_id=1, source_target_pairs={{0,0},{1,128},{2,256},{3,384},{4,4},{5,132},{6,260},{7,388},{8,32}... | collective-permute-start | bytes 98312 | tf_op jit(solution)/shard_map/ppermute | solution.py:197
  8.7 26.2 %all-to-all-start = ((s32[32,1,128]{2,1,0:T(1,128)}), s32[32,1,128]{2,1,0:T(1,128)S(1)}, u32[]{:S(2)}, u32[]{:S(2)}) async-start(s32[32,1,128]{2,1,0:T(1,128)} %bitcast.3), calls=%async_computation | async-start | bytes 32768 | tf_op jit(solution)/shard_map/all_to_all | solution.py:200
  28.1 10.2 %collective-permute-start.2 = (bf16[224,512]{1,0:T(8,128)(2,1)}, bf16[224,512]{1,0:T(8,128)(2,1)S(1)}, u32[]{:S(2)}, u32[]{:S(2)}) collective-permute-start(bf16[224,512]{1,0:T(8,128)(2,1)} %bitcast.10), channel_id=1, source_target_pairs={{0,32},{32,0},{64,96},{96,64},{1,33},{33,1},{65,97},{97,65},{2,34}... | collective-permute-start | bytes 688136 | tf_op jit(solution)/shard_map/ppermute | solution.py:188
  34.9 8.4 %collective-permute-start.3 = (bf16[224,512]{1,0:T(8,128)(2,1)S(1)}, bf16[224,512]{1,0:T(8,128)(2,1)S(1)}, u32[]{:S(2)}, u32[]{:S(2)}) collective-permute-start(bf16[224,512]{1,0:T(8,128)(2,1)S(1)} %collective-permute-done.refs_2_), channel_id=1, source_target_pairs={{0,32},{32,0},{64,96},{96,64},{1,33},{33,1},{65,97},{97,65},{2,34}... | collective-permute-start | bytes 688136 | tf_op jit(solution)/shard_map/ppermute | solution.py:188
  43.3 0.9 copy-start.1
  46.5 24.2 %all-to-all-start.1 = ((bf16[32,4,16,224]{3,2,1,0:T(8,128)(2,1)}), bf16[32,4,16,224]{3,2,1,0:T(8,128)(2,1)S(1)}, u32[]{:S(2)}, u32[]{:S(2)}) async-start(bf16[32,4,16,224]{3,2,1,0:T(8,128)(2,1)} %pick.1), calls=%async_computation.1 | async-start | bytes 2097152 | tf_op jit(solution)/shard_map/all_to_all | solution.py:204
  71.4 40.4 %copy-start = (bf16[2,896,512]{2,1,0:T(8,128)(2,1)S(1)}, bf16[2,896,512]{2,1,0:T(8,128)(2,1)}, u32[]{:S(2)}) copy-start(bf16[2,896,512]{2,1,0:T(8,128)(2,1)} %kv_ref.1) | copy-start | bytes 5505028
  71.5 40.4 %copy-start.2 = (bf16[128,512]{1,0:T(8,128)(2,1)S(1)}, bf16[128,512]{1,0:T(8,128)(2,1)}, u32[]{:S(2)}) copy-start(bf16[128,512]{1,0:T(8,128)(2,1)} %q_ref.1) | copy-start | bytes 393220
  71.5 70.1 %all-to-all-start.2 = ((bf16[16,256,512]{2,1,0:T(8,128)(2,1)}), bf16[16,256,512]{2,1,0:T(8,128)(2,1)}, u32[]{:S(2)}, u32[]{:S(2)}) async-start(bf16[16,256,512]{2,1,0:T(8,128)(2,1)} %broadcast_in_dim.30), calls=%async_computation.2 | async-start | bytes 8388608 | tf_op jit(solution)/shard_map/all_to_all | solution.py:214

commit v6 on v5

--- a/solution.py
+++ b/solution.py
@@ -52,22 +52,28 @@
     keys = keys.astype(jnp.bfloat16)
     values = jnp.dot(feats, kv_ref[1], preferred_element_type=jnp.float32)
     values = values.astype(jnp.bfloat16)
+    scale = 1.0 / math.sqrt(HEAD)
+    units = []
     for span in range(spans):
         for head in range(heads):
             tokens = slice(span * SPAN, (span + 1) * SPAN)
             rows = slice(span * per_span, (span + 1) * per_span)
-            lanes = slice(head * HEAD, (head + 1) * HEAD)
-            scores = lax.dot_general(
-                q_ref[tokens, lanes], keys[rows, lanes], LAST_DIMS,
-                preferred_element_type=jnp.float32,
-            ) * (1.0 / math.sqrt(HEAD))
-            exponent = jnp.exp(scores - jnp.max(scores, axis=-1, keepdims=True))
-            weights = exponent / jnp.sum(exponent, axis=-1, keepdims=True)
-            mixed = jnp.dot(
-                weights.astype(jnp.bfloat16), values[rows, lanes],
-                preferred_element_type=jnp.float32,
-            )
-            mixed_ref[tokens, lanes] = mixed.astype(jnp.bfloat16)
+            units.append((tokens, rows, slice(head * HEAD, (head + 1) * HEAD)))
+    scores = [
+        lax.dot_general(
+            q_ref[tokens, lanes], keys[rows, lanes], LAST_DIMS,
+            preferred_element_type=jnp.float32,
+        ) * scale
+        for tokens, rows, lanes in units
+    ]
+    weights = []
+    for score in scores:
+        exponent = jnp.exp(score - jnp.max(score, axis=-1, keepdims=True))
+        weight = exponent / jnp.sum(exponent, axis=-1, keepdims=True)
+        weights.append(weight.astype(jnp.bfloat16))
+    for weight, (tokens, rows, lanes) in zip(weights, units):
+        mixed = jnp.dot(weight, values[rows, lanes], preferred_element_type=jnp.float32)
+        mixed_ref[tokens, lanes] = mixed.astype(jnp.bfloat16)
 
 
 def attend(queries, feats, kv_weight):
@@ -200,6 +206,8 @@
     served = lax.all_to_all(wanted, PEERS, split_axis=0, concat_axis=0, tiled=True)
     one, two = from_z(feats, 1), from_z(feats, 2)
     two, served, piece = lax.optimization_barrier((two, served, piece))
+    slots = slot_of(nbr_map // enc_blocks)
+    one, slots = lax.optimization_barrier((one, slots))
     chosen = pick(my_z, served, [feats, one, two, from_z(two, 1)])
     arrived = lax.all_to_all(chosen, PEERS, split_axis=0, concat_axis=0, tiled=True)
 
@@ -207,7 +215,6 @@
     four = lax.all_gather(piece, ("z", "c"), axis=0, tiled=True)
     pieces = jnp.broadcast_to(four[None], (NY * NX,) + four.shape)
 
-    slots = slot_of(nbr_map // enc_blocks)
     slots, pieces = lax.optimization_barrier((slots, pieces))
     gathered = take(slots, arrived.reshape(-1, ROWBLK, features))
     gathered, pieces = lax.optimization_barrier((gathered, pieces))

time: 147 us -> 146 us (level)
  blocking collectives: 68.4 us -> 71.2 us
  Pallas kernels: 10.4 us -> 8.56 us
    all_gather x1, blocking collectives: 20.7 us -> 23.5 us  [shards(): mixed = lax.all_gather(mixed, 't', axis=0, tiled=False)]
    pallas_call x1, Pallas kernels: 3.55 us -> 1.75 us  [attend(): pl.pallas_call(attend_kernel, in_specs=[IN_VMEM, IN_VMEM, IN_VMEM], out_s...]
  transfers between devices with their start and end apart: 7 -> 7, of which waited for: 3 -> 4; matrix products, arithmetic and copies ran while one was open for 3% -> 3% of each run, Pallas kernels for 2% -> 1%
where the time goes in v6:
time: 146 us; the launch traced here: 145 us
  blocking collectives  71.2 us (49%)
  starting transfers between devices  46.4 us (32%)
  waiting for transfers between devices  12.9 us (9%)
  Pallas kernels  8.56 us (6%)
  local copies, waits for them, and re-layouts  3.31 us (2%)
  other arithmetic  2.25 us (2%)
    all_gather x1, blocking collectives, shards(): feats = lax.all_gather(gathered, 't', axis=0, tiled=True)  33.4 us
    all_gather x1, blocking collectives, shards(): mixed = lax.all_gather(mixed, 't', axis=0, tiled=False)  23.5 us
    all_to_all x1, starting transfers between devices, shards(): lax.all_to_all(wanted, PEERS, split_axis=0, concat_axis=0, tiled=True)  19.4 us
    all_gather x1, blocking collectives, shards(): four = lax.all_gather(piece, ('z', 'c'), axis=0, tiled=True)  14.3 us
    ppermute x3, starting transfers between devices, from_z(): return lax.ppermute(value, 'z', [(z, z ^ bits) for z in range(NZ)])  12.3 us
    all_to_all x1, starting transfers between devices, shards(): lax.all_to_all(chosen, PEERS, split_axis=0, concat_axis=0, tiled=True)  6.8 us
    all_to_all x1, starting transfers between devices, shards(): lax.all_to_all(pieces, ('y', 'x'), split_axis=0, concat_axis=0, tiled=True)  6.56 us
    ppermute x3, waiting for transfers between devices, from_z(): return lax.ppermute(value, 'z', [(z, z ^ bits) for z in range(NZ)])  4.39 us
  transfers between devices with their start and end apart: 7, of which 4 were waited for; matrix products, arithmetic and copies ran while one was open for 3% of the time, Pallas kernels for 1%

profile of v6, /device:TPU:1, one launch (start us, length us, event | category | flops | bytes accessed | tf_op | source)
XLA Modules:
  0.0 144.7 jit_solution(8034050394093174141)
XLA Ops:
  0.0 5.7 %collective-permute-start.1 = (bf16[224,512]{1,0:T(8,128)(2,1)}, bf16[224,512]{1,0:T(8,128)(2,1)S(1)}, u32[]{:S(2)}, u32[]{:S(2)}) collective-permute-start(bf16[224,512]{1,0:T(8,128)(2,1)} %bitcast.9), channel_id=1, source_target_pairs={{0,64},{32,96},{64,0},{96,32},{1,65},{33,97},{65,1},{97,33},{2,66}... | collective-permute-start | bytes 688136 | tf_op jit(solution)/shard_map/ppermute | solution.py:194
  5.8 0.1 select_multiply_fusion
  5.8 1.5 %fusion = s32[32,128]{1,0:T(8,128)} fusion(s32[32,128]{1,0:T(8,128)S(1)} %select_multiply_fusion, s32[2,16]{1,0:T(2,128)} %param.9), kind=kLoop, calls=%fused_computation.3 | loop fusion | flops 782336 | bytes 32896 | tf_op jit(solution)/shard_map/reduce_sum | solution.py:43
  7.3 1.4 collective-permute-start.2
  8.7 19.4 %all-to-all-start = ((s32[32,1,128]{2,1,0:T(1,128)}), s32[32,1,128]{2,1,0:T(1,128)S(1)}, u32[]{:S(2)}, u32[]{:S(2)}) async-start(s32[32,1,128]{2,1,0:T(1,128)} %bitcast.3), calls=%async_computation | async-start | bytes 32768 | tf_op jit(solution)/shard_map/all_to_all | solution.py:206
  28.1 3.3 %collective-permute-start = (bf16[224,512]{1,0:T(8,128)(2,1)}, bf16[224,512]{1,0:T(8,128)(2,1)S(1)}, u32[]{:S(2)}, u32[]{:S(2)}) collective-permute-start(bf16[224,512]{1,0:T(8,128)(2,1)} %bitcast.10), channel_id=1, source_target_pairs={{0,32},{32,0},{64,96},{96,64},{1,33},{33,1},{65,97},{97,65},{2,34}... | collective-permute-start | bytes 688136 | tf_op jit(solution)/shard_map/ppermute | solution.py:194
  31.4 3.6 %all-to-all-done.served_ref = s32[32,1,128]{2,1,0:T(1,128)S(1)} async-done(((s32[32,1,128]{2,1,0:T(1,128)}), s32[32,1,128]{2,1,0:T(1,128)S(1)}, u32[]{:S(2)}, u32[]{:S(2)}) %all-to-all-start) | async-done | bytes 16416 | tf_op jit(solution)/shard_map/all_to_all | solution.py:206
  34.9 3.3 %collective-permute-start.3 = (bf16[224,512]{1,0:T(8,128)(2,1)S(1)}, bf16[224,512]{1,0:T(8,128)(2,1)S(1)}, u32[]{:S(2)}, u32[]{:S(2)}) collective-permute-start(bf16[224,512]{1,0:T(8,128)(2,1)S(1)} %collective-permute-done.1.refs_2_), channel_id=1, source_target_pairs={{0,32},{32,0},{64,96},{96,64},{1,33},{33,1},{65,97},{97,65},{2,34}... | collective-permute-start | bytes 688136 | tf_op jit(solution)/shard_map/ppermute | solution.py:194
  38.2 0.7 fusion.2.slot_ref
  38.9 4.4 %collective-permute-done.3.refs_3_ = bf16[224,512]{1,0:T(8,128)(2,1)S(1)} collective-permute-done((bf16[224,512]{1,0:T(8,128)(2,1)S(1)}, bf16[224,512]{1,0:T(8,128)(2,1)S(1)}, u32[]{:S(2)}, u32[]{:S(2)}) %collective-permute-start.3) | collective-permute-done | bytes 229408 | tf_op jit(solution)/shard_map/ppermute | solution.py:194
  43.3 0.9 copy-done.1
  44.3 2.3 %pick.1 = bf16[32,4,16,224]{3,2,1,0:T(8,128)(2,1)} custom-call(s32[1]{0:T(128)} %bitcast.1.z_ref, s32[32,1,128]{2,1,0:T(1,128)S(1)} %all-to-all-done.served_ref, bf16[224,512]{1,0:T(8,128)(2,1)S(1)} %bitcast.11, bf16[224,512]{1,0:T(8,128)(2,1)S(1)} %collective-permute-done.refs_1_, bf16[224,512]{1,0:T(8,128)(2,1)S(1)} %collective-permute-done.1.refs_2_, ...), custom_call_target="tpu_custom_call" | custom-call | tf_op jit(solution)/shard_map/pick/pallas_call | solution.py:104
  46.5 6.8 %all-to-all-start.1 = ((bf16[32,4,16,224]{3,2,1,0:T(8,128)(2,1)}), bf16[32,4,16,224]{3,2,1,0:T(8,128)(2,1)S(1)}, u32[]{:S(2)}, u32[]{:S(2)}) async-start(bf16[32,4,16,224]{3,2,1,0:T(8,128)(2,1)} %pick.1), calls=%async_computation.1 | async-start | bytes 2097152 | tf_op jit(solution)/shard_map/all_to_all | solution.py:212
  53.3 14.3 %all_gather.12 = bf16[256,512]{1,0:T(8,128)(2,1)S(1)} all-gather(bf16[32,512]{1,0:T(8,128)(2,1)S(1)} %collective-permute-done.2), channel_id=1, replica_groups=mesh['y'=4,'z'=4,'x'=4,'c'=2,'t'=4] {'z','c'}, dimensions={0}, use_global_device_ids=true | all-gather | bytes 294912 | tf_op jit(solution)/shard_map/all_gather | solution.py:215
  67.6 2.4 %broadcast_in_dim.30 = bf16[16,256,512]{2,1,0:T(8,128)(2,1)} broadcast(bf16[256,512]{1,0:T(8,128)(2,1)S(1)} %all_gather.12), dimensions={1,2} | broadcast | bytes 4456448 | tf_op jit(solution)/shard_map/broadcast_in_dim | solution.py:216
  70.0 0.5 all-to-all-done.1
  70.5 0.7 take.1
  71.2 0.0 copy-start
  71.2 6.6 %all-to-all-start.2 = ((bf16[16,256,512]{2,1,0:T(8,128)(2,1)}), bf16[16,256,512]{2,1,0:T(8,128)(2,1)}, u32[]{:S(2)}, u32[]{:S(2)}) async-start(bf16[16,256,512]{2,1,0:T(8,128)(2,1)} %broadcast_in_dim.30), calls=%async_computation.2 | async-start | bytes 8388608 | tf_op jit(solution)/shard_map/all_to_all | solution.py:221
  77.8 33.4 %all_gather.13.feat_ref = bf16[896,512]{1,0:T(8,128)(2,1)S(1)} all-gather(bf16[224,512]{1,0:T(8,128)(2,1)S(1)} %take.1), channel_id=1, replica_groups=mesh['y'=4,'z'=4,'x'=4,'c'=2,'t'=4] {'t'}, dimensions={0}, use_global_device_ids=true | all-gather | bytes 1146880 | tf_op jit(solution)/shard_map/all_gather | solution.py:223
  111.2 1.8 %attend.1 = bf16[128,512]{1,0:T(8,128)(2,1)S(1)} custom-call(bf16[128,512]{1,0:T(8,128)(2,1)S(1)} %copy-done.2, bf16[896,512]{1,0:T(8,128)(2,1)S(1)} %all_gather.13.feat_ref, bf16[2,896,512]{2,1,0:T(8,128)(2,1)S(1)} %copy-done), custom_call_target="tpu_custom_call" | custom-call | tf_op jit(solution)/shard_map/attend/pallas_call | solution.py:80
  112.9 23.5 %all-gather = bf16[512,512]{1,0:T(8,128)(2,1)S(1)} all-gather(bf16[128,512]{1,0:T(8,128)(2,1)S(1)} %attend.1), channel_id=2, replica_groups=mesh['y'=4,'z'=4,'x'=4,'c'=2,'t'=4] {'t'}, dimensions={0}, use_global_device_ids=true | all-gather | bytes 655360 | tf_op jit(solution)/shard_map/all_gather | solution.py:226
  136.4 4.4 %all-to-all-done.2 = bf16[16,256,512]{2,1,0:T(8,128)(2,1)} async-done(((bf16[16,256,512]{2,1,0:T(8,128)(2,1)}), bf16[16,256,512]{2,1,0:T(8,128)(2,1)}, u32[]{:S(2)}, u32[]{:S(2)}) %all-to-all-start.2) | async-done | bytes 4194336 | tf_op jit(solution)/shard_map/all_to_all | solution.py:221
  140.8 3.9 %project.1 = bf16[128,1024]{1,0:T(8,128)(2,1)} custom-call(bf16[4,128,512]{2,1,0:T(8,128)(2,1)S(1)} %bitcast.8, bf16[4,1024,512]{2,1,0:T(8,128)(2,1)} %bitcast.6.far_ref), custom_call_target="tpu_custom_call" | custom-call | tf_op jit(solution)/shard_map/project/pallas_call | solution.py:163
  (9 shorter events, 0.0 us)
Async XLA Ops:
  0.0 34.9 %collective-permute-start.1 = (bf16[224,512]{1,0:T(8,128)(2,1)}, bf16[224,512]{1,0:T(8,128)(2,1)S(1)}, u32[]{:S(2)}, u32[]{:S(2)}) collective-permute-start(bf16[224,512]{1,0:T(8,128)(2,1)} %bitcast.9), channel_id=1, source_target_pairs={{0,64},{32,96},{64,0},{96,32},{1,65},{33,97},{65,1},{97,33},{2,66}... | collective-permute-start | bytes 688136 | tf_op jit(solution)/shard_map/ppermute | solution.py:194
  7.3 27.7 %collective-permute-start.2 = (bf16[32,512]{1,0:T(8,128)(2,1)}, bf16[32,512]{1,0:T(8,128)(2,1)S(1)}, u32[]{:S(2)}, u32[]{:S(2)}) collective-permute-start(bf16[32,512]{1,0:T(8,128)(2,1)} %bitcast.12), channel_id=1, source_target_pairs={{0,0},{1,128},{2,256},{3,384},{4,4},{5,132},{6,260},{7,388},{8,32}... | collective-permute-start | bytes 98312 | tf_op jit(solution)/shard_map/ppermute | solution.py:203
  8.7 26.2 %all-to-all-start = ((s32[32,1,128]{2,1,0:T(1,128)}), s32[32,1,128]{2,1,0:T(1,128)S(1)}, u32[]{:S(2)}, u32[]{:S(2)}) async-start(s32[32,1,128]{2,1,0:T(1,128)} %bitcast.3), calls=%async_computation | async-start | bytes 32768 | tf_op jit(solution)/shard_map/all_to_all | solution.py:206
  28.1 10.9 %collective-permute-start = (bf16[224,512]{1,0:T(8,128)(2,1)}, bf16[224,512]{1,0:T(8,128)(2,1)S(1)}, u32[]{:S(2)}, u32[]{:S(2)}) collective-permute-start(bf16[224,512]{1,0:T(8,128)(2,1)} %bitcast.10), channel_id=1, source_target_pairs={{0,32},{32,0},{64,96},{96,64},{1,33},{33,1},{65,97},{97,65},{2,34}... | collective-permute-start | bytes 688136 | tf_op jit(solution)/shard_map/ppermute | solution.py:194
  34.9 8.4 %collective-permute-start.3 = (bf16[224,512]{1,0:T(8,128)(2,1)S(1)}, bf16[224,512]{1,0:T(8,128)(2,1)S(1)}, u32[]{:S(2)}, u32[]{:S(2)}) collective-permute-start(bf16[224,512]{1,0:T(8,128)(2,1)S(1)} %collective-permute-done.1.refs_2_), channel_id=1, source_target_pairs={{0,32},{32,0},{64,96},{96,64},{1,33},{33,1},{65,97},{97,65},{2,34}... | collective-permute-start | bytes 688136 | tf_op jit(solution)/shard_map/ppermute | solution.py:194
  43.3 0.9 copy-start.1
  46.5 24.0 %all-to-all-start.1 = ((bf16[32,4,16,224]{3,2,1,0:T(8,128)(2,1)}), bf16[32,4,16,224]{3,2,1,0:T(8,128)(2,1)S(1)}, u32[]{:S(2)}, u32[]{:S(2)}) async-start(bf16[32,4,16,224]{3,2,1,0:T(8,128)(2,1)} %pick.1), calls=%async_computation.1 | async-start | bytes 2097152 | tf_op jit(solution)/shard_map/all_to_all | solution.py:212
  71.2 40.0 %copy-start = (bf16[2,896,512]{2,1,0:T(8,128)(2,1)S(1)}, bf16[2,896,512]{2,1,0:T(8,128)(2,1)}, u32[]{:S(2)}) copy-start(bf16[2,896,512]{2,1,0:T(8,128)(2,1)} %kv_ref.1) | copy-start | bytes 5505028
  71.2 40.0 %copy-start.2 = (bf16[128,512]{1,0:T(8,128)(2,1)S(1)}, bf16[128,512]{1,0:T(8,128)(2,1)}, u32[]{:S(2)}) copy-start(bf16[128,512]{1,0:T(8,128)(2,1)} %q_ref.1) | copy-start | bytes 393220
  71.2 69.6 %all-to-all-start.2 = ((bf16[16,256,512]{2,1,0:T(8,128)(2,1)}), bf16[16,256,512]{2,1,0:T(8,128)(2,1)}, u32[]{:S(2)}, u32[]{:S(2)}) async-start(bf16[16,256,512]{2,1,0:T(8,128)(2,1)} %broadcast_in_dim.30), calls=%async_computation.2 | async-start | bytes 8388608 | tf_op jit(solution)/shard_map/all_to_all | solution.py:221

commit v7 on v6

--- a/solution.py
+++ b/solution.py
@@ -111,22 +111,21 @@
     )(my_z, served, *held)
 
 
-def take_kernel(slot_ref, arrived_ref, feats_ref, rows_ref):
+def take_kernel(slot_ref, arrived_ref, rows_ref):
     spans, per_span = slot_ref.shape
     for span in range(spans):
         for at in range(per_span):
             to = (span * per_span + at) * ROWBLK
             rows_ref[to : to + ROWBLK] = arrived_ref[slot_ref[span, at]]
-    feats_ref[...] = rows_ref[...].T
 
 
 def take(slots, arrived):
-    rows, features = slots.size * ROWBLK, arrived.shape[2]
     return pl.pallas_call(
         take_kernel,
         in_specs=[IN_SMEM, IN_VMEM],
-        out_shape=jax.ShapeDtypeStruct((features, rows), arrived.dtype),
-        scratch_shapes=[pltpu.VMEM((rows, features), arrived.dtype)],
+        out_shape=jax.ShapeDtypeStruct(
+            (slots.size * ROWBLK, arrived.shape[2]), arrived.dtype
+        ),
         compiler_params=PARAMS,
         name="take",
     )(slots, arrived)
@@ -220,7 +219,7 @@
     gathered, pieces = lax.optimization_barrier((gathered, pieces))
     w_cols = lax.all_to_all(pieces, ("y", "x"), split_axis=0, concat_axis=0, tiled=True)
     w_cols = w_cols.reshape(NY, -1, w_cols.shape[2])
-    feats = lax.all_gather(gathered, "t", axis=0, tiled=True)
+    feats = lax.all_gather(gathered.T, "t", axis=0, tiled=True)
 
     mixed = attend(queries, feats, kv_weight)
     mixed = lax.all_gather(mixed, "t", axis=0, tiled=False)

time: 146 us -> 146 us (level)
  blocking collectives: 71.2 us -> 64.8 us
  waiting for transfers between devices: 12.9 us -> 19.1 us
    all_to_all x1, waiting for transfers between devices: 4.39 us -> 10.7 us  [shards(): lax.all_to_all(pieces, ('y', 'x'), split_axis=0, concat_axis=0, tiled=True)]
    all_gather x1, blocking collectives: 23.5 us -> 19.4 us  [shards(): mixed = lax.all_gather(mixed, 't', axis=0, tiled=False)]
    all_gather x1, blocking collectives: 33.4 us -> 31.1 us  [shards(): feats = lax.all_gather(gathered.T, 't', axis=0, tiled=True)]
where the time goes in v7:
time: 146 us; the launch traced here: 145 us
  blocking collectives  64.8 us (44%)
  starting transfers between devices  46.4 us (32%)
  waiting for transfers between devices  19.1 us (13%)
  Pallas kernels  8.46 us (6%)
  local copies, waits for them, and re-layouts  3.45 us (2%)
  other arithmetic  2.25 us (2%)
    all_gather x1, blocking collectives, shards(): feats = lax.all_gather(gathered.T, 't', axis=0, tiled=True)  31.1 us
    all_to_all x1, starting transfers between devices, shards(): lax.all_to_all(wanted, PEERS, split_axis=0, concat_axis=0, tiled=True)  19.4 us
    all_gather x1, blocking collectives, shards(): mixed = lax.all_gather(mixed, 't', axis=0, tiled=False)  19.4 us
    all_gather x1, blocking collectives, shards(): four = lax.all_gather(piece, ('z', 'c'), axis=0, tiled=True)  14.3 us
    ppermute x3, starting transfers between devices, from_z(): return lax.ppermute(value, 'z', [(z, z ^ bits) for z in range(NZ)])  12.3 us
    all_to_all x1, waiting for transfers between devices, shards(): lax.all_to_all(pieces, ('y', 'x'), split_axis=0, concat_axis=0, tiled=True)  10.7 us
    all_to_all x1, starting transfers between devices, shards(): lax.all_to_all(chosen, PEERS, split_axis=0, concat_axis=0, tiled=True)  6.8 us
    all_to_all x1, starting transfers between devices, shards(): lax.all_to_all(pieces, ('y', 'x'), split_axis=0, concat_axis=0, tiled=True)  6.56 us
  transfers between devices with their start and end apart: 7, of which 4 were waited for; matrix products, arithmetic and copies ran while one was open for 3% of the time, Pallas kernels for 1%

profile of v7, /device:TPU:1, one launch (start us, length us, event | category | flops | bytes accessed | tf_op | source)
XLA Modules:
  0.0 144.6 jit_solution(10542480523869974776)
XLA Ops:
  0.0 5.7 %collective-permute-start.1 = (bf16[224,512]{1,0:T(8,128)(2,1)}, bf16[224,512]{1,0:T(8,128)(2,1)S(1)}, u32[]{:S(2)}, u32[]{:S(2)}) collective-permute-start(bf16[224,512]{1,0:T(8,128)(2,1)} %bitcast.10), channel_id=1, source_target_pairs={{0,64},{32,96},{64,0},{96,32},{1,65},{33,97},{65,1},{97,33},{2,66}... | collective-permute-start | bytes 688136 | tf_op jit(solution)/shard_map/ppermute | solution.py:193
  5.8 0.1 select_multiply_fusion
  5.8 1.5 %fusion = s32[32,128]{1,0:T(8,128)} fusion(s32[32,128]{1,0:T(8,128)S(1)} %select_multiply_fusion, s32[2,16]{1,0:T(2,128)} %param.9), kind=kLoop, calls=%fused_computation.3 | loop fusion | flops 782336 | bytes 32896 | tf_op jit(solution)/shard_map/reduce_sum | solution.py:43
  7.3 1.4 collective-permute-start.2
  8.7 19.4 %all-to-all-start = ((s32[32,1,128]{2,1,0:T(1,128)}), s32[32,1,128]{2,1,0:T(1,128)S(1)}, u32[]{:S(2)}, u32[]{:S(2)}) async-start(s32[32,1,128]{2,1,0:T(1,128)} %bitcast.3), calls=%async_computation | async-start | bytes 32768 | tf_op jit(solution)/shard_map/all_to_all | solution.py:205
  28.1 3.3 %collective-permute-start = (bf16[224,512]{1,0:T(8,128)(2,1)}, bf16[224,512]{1,0:T(8,128)(2,1)S(1)}, u32[]{:S(2)}, u32[]{:S(2)}) collective-permute-start(bf16[224,512]{1,0:T(8,128)(2,1)} %bitcast.11), channel_id=1, source_target_pairs={{0,32},{32,0},{64,96},{96,64},{1,33},{33,1},{65,97},{97,65},{2,34}... | collective-permute-start | bytes 688136 | tf_op jit(solution)/shard_map/ppermute | solution.py:193
  31.4 3.6 %all-to-all-done.served_ref = s32[32,1,128]{2,1,0:T(1,128)S(1)} async-done(((s32[32,1,128]{2,1,0:T(1,128)}), s32[32,1,128]{2,1,0:T(1,128)S(1)}, u32[]{:S(2)}, u32[]{:S(2)}) %all-to-all-start) | async-done | bytes 16416 | tf_op jit(solution)/shard_map/all_to_all | solution.py:205
  34.9 3.3 %collective-permute-start.3 = (bf16[224,512]{1,0:T(8,128)(2,1)S(1)}, bf16[224,512]{1,0:T(8,128)(2,1)S(1)}, u32[]{:S(2)}, u32[]{:S(2)}) collective-permute-start(bf16[224,512]{1,0:T(8,128)(2,1)S(1)} %collective-permute-done.1.refs_2_), channel_id=1, source_target_pairs={{0,32},{32,0},{64,96},{96,64},{1,33},{33,1},{65,97},{97,65},{2,34}... | collective-permute-start | bytes 688136 | tf_op jit(solution)/shard_map/ppermute | solution.py:193
  38.2 0.7 fusion.2.slot_ref
  38.9 4.4 %collective-permute-done.3.refs_3_ = bf16[224,512]{1,0:T(8,128)(2,1)S(1)} collective-permute-done((bf16[224,512]{1,0:T(8,128)(2,1)S(1)}, bf16[224,512]{1,0:T(8,128)(2,1)S(1)}, u32[]{:S(2)}, u32[]{:S(2)}) %collective-permute-start.3) | collective-permute-done | bytes 229408 | tf_op jit(solution)/shard_map/ppermute | solution.py:193
  43.3 0.9 copy-done.1
  44.3 2.3 %pick.1 = bf16[32,4,16,224]{3,2,1,0:T(8,128)(2,1)} custom-call(s32[1]{0:T(128)} %bitcast.1.z_ref, s32[32,1,128]{2,1,0:T(1,128)S(1)} %all-to-all-done.served_ref, bf16[224,512]{1,0:T(8,128)(2,1)S(1)} %bitcast.12, bf16[224,512]{1,0:T(8,128)(2,1)S(1)} %collective-permute-done.refs_1_, bf16[224,512]{1,0:T(8,128)(2,1)S(1)} %collective-permute-done.1.refs_2_, ...), custom_call_target="tpu_custom_call" | custom-call | tf_op jit(solution)/shard_map/pick/pallas_call | solution.py:104
  46.5 6.8 %all-to-all-start.1 = ((bf16[32,4,16,224]{3,2,1,0:T(8,128)(2,1)}), bf16[32,4,16,224]{3,2,1,0:T(8,128)(2,1)S(1)}, u32[]{:S(2)}, u32[]{:S(2)}) async-start(bf16[32,4,16,224]{3,2,1,0:T(8,128)(2,1)} %pick.1), calls=%async_computation.1 | async-start | bytes 2097152 | tf_op jit(solution)/shard_map/all_to_all | solution.py:211
  53.3 14.3 %all_gather.12 = bf16[256,512]{1,0:T(8,128)(2,1)S(1)} all-gather(bf16[32,512]{1,0:T(8,128)(2,1)S(1)} %collective-permute-done.2), channel_id=1, replica_groups=mesh['y'=4,'z'=4,'x'=4,'c'=2,'t'=4] {'z','c'}, dimensions={0}, use_global_device_ids=true | all-gather | bytes 294912 | tf_op jit(solution)/shard_map/all_gather | solution.py:214
  67.6 2.4 %broadcast_in_dim.30 = bf16[16,256,512]{2,1,0:T(8,128)(2,1)} broadcast(bf16[256,512]{1,0:T(8,128)(2,1)S(1)} %all_gather.12), dimensions={1,2} | broadcast | bytes 4456448 | tf_op jit(solution)/shard_map/broadcast_in_dim | solution.py:215
  70.0 0.5 all-to-all-done.1
  70.5 0.6 take.1
  71.1 6.6 %all-to-all-start.2 = ((bf16[16,256,512]{2,1,0:T(8,128)(2,1)}), bf16[16,256,512]{2,1,0:T(8,128)(2,1)}, u32[]{:S(2)}, u32[]{:S(2)}) async-start(bf16[16,256,512]{2,1,0:T(8,128)(2,1)} %broadcast_in_dim.30), calls=%async_computation.2 | async-start | bytes 8388608 | tf_op jit(solution)/shard_map/all_to_all | solution.py:220
  77.7 0.1 copy.7
  77.8 31.1 %all_gather.13.feat_ref = bf16[896,512]{1,0:T(8,128)(2,1)S(1)} all-gather(bf16[224,512]{1,0:T(8,128)(2,1)S(1)} %bitcast.13), channel_id=1, replica_groups=mesh['y'=4,'z'=4,'x'=4,'c'=2,'t'=4] {'t'}, dimensions={0}, use_global_device_ids=true | all-gather | bytes 1146880 | tf_op jit(solution)/shard_map/all_gather | solution.py:222
  108.9 1.7 %attend.1 = bf16[128,512]{1,0:T(8,128)(2,1)S(1)} custom-call(bf16[128,512]{1,0:T(8,128)(2,1)S(1)} %copy-done.2, bf16[896,512]{1,0:T(8,128)(2,1)S(1)} %all_gather.13.feat_ref, bf16[2,896,512]{2,1,0:T(8,128)(2,1)S(1)} %copy-done), custom_call_target="tpu_custom_call" | custom-call | tf_op jit(solution)/shard_map/attend/pallas_call | solution.py:80
  110.7 19.4 %all-gather = bf16[512,512]{1,0:T(8,128)(2,1)S(1)} all-gather(bf16[128,512]{1,0:T(8,128)(2,1)S(1)} %attend.1), channel_id=2, replica_groups=mesh['y'=4,'z'=4,'x'=4,'c'=2,'t'=4] {'t'}, dimensions={0}, use_global_device_ids=true | all-gather | bytes 655360 | tf_op jit(solution)/shard_map/all_gather | solution.py:225
  130.1 10.7 %all-to-all-done.2 = bf16[16,256,512]{2,1,0:T(8,128)(2,1)} async-done(((bf16[16,256,512]{2,1,0:T(8,128)(2,1)}), bf16[16,256,512]{2,1,0:T(8,128)(2,1)}, u32[]{:S(2)}, u32[]{:S(2)}) %all-to-all-start.2) | async-done | bytes 4194336 | tf_op jit(solution)/shard_map/all_to_all | solution.py:220
  140.7 3.9 %project.1 = bf16[128,1024]{1,0:T(8,128)(2,1)} custom-call(bf16[4,128,512]{2,1,0:T(8,128)(2,1)S(1)} %bitcast.9, bf16[4,1024,512]{2,1,0:T(8,128)(2,1)} %bitcast.7.far_ref), custom_call_target="tpu_custom_call" | custom-call | tf_op jit(solution)/shard_map/project/pallas_call | solution.py:162
  (10 shorter events, 0.0 us)
Async XLA Ops:
  0.0 34.9 %collective-permute-start.1 = (bf16[224,512]{1,0:T(8,128)(2,1)}, bf16[224,512]{1,0:T(8,128)(2,1)S(1)}, u32[]{:S(2)}, u32[]{:S(2)}) collective-permute-start(bf16[224,512]{1,0:T(8,128)(2,1)} %bitcast.10), channel_id=1, source_target_pairs={{0,64},{32,96},{64,0},{96,32},{1,65},{33,97},{65,1},{97,33},{2,66}... | collective-permute-start | bytes 688136 | tf_op jit(solution)/shard_map/ppermute | solution.py:193
  7.3 27.7 %collective-permute-start.2 = (bf16[32,512]{1,0:T(8,128)(2,1)}, bf16[32,512]{1,0:T(8,128)(2,1)S(1)}, u32[]{:S(2)}, u32[]{:S(2)}) collective-permute-start(bf16[32,512]{1,0:T(8,128)(2,1)} %bitcast.14), channel_id=1, source_target_pairs={{0,0},{1,128},{2,256},{3,384},{4,4},{5,132},{6,260},{7,388},{8,32}... | collective-permute-start | bytes 98312 | tf_op jit(solution)/shard_map/ppermute | solution.py:202
  8.7 26.2 %all-to-all-start = ((s32[32,1,128]{2,1,0:T(1,128)}), s32[32,1,128]{2,1,0:T(1,128)S(1)}, u32[]{:S(2)}, u32[]{:S(2)}) async-start(s32[32,1,128]{2,1,0:T(1,128)} %bitcast.3), calls=%async_computation | async-start | bytes 32768 | tf_op jit(solution)/shard_map/all_to_all | solution.py:205
  28.1 10.9 %collective-permute-start = (bf16[224,512]{1,0:T(8,128)(2,1)}, bf16[224,512]{1,0:T(8,128)(2,1)S(1)}, u32[]{:S(2)}, u32[]{:S(2)}) collective-permute-start(bf16[224,512]{1,0:T(8,128)(2,1)} %bitcast.11), channel_id=1, source_target_pairs={{0,32},{32,0},{64,96},{96,64},{1,33},{33,1},{65,97},{97,65},{2,34}... | collective-permute-start | bytes 688136 | tf_op jit(solution)/shard_map/ppermute | solution.py:193
  34.9 8.4 %collective-permute-start.3 = (bf16[224,512]{1,0:T(8,128)(2,1)S(1)}, bf16[224,512]{1,0:T(8,128)(2,1)S(1)}, u32[]{:S(2)}, u32[]{:S(2)}) collective-permute-start(bf16[224,512]{1,0:T(8,128)(2,1)S(1)} %collective-permute-done.1.refs_2_), channel_id=1, source_target_pairs={{0,32},{32,0},{64,96},{96,64},{1,33},{33,1},{65,97},{97,65},{2,34}... | collective-permute-start | bytes 688136 | tf_op jit(solution)/shard_map/ppermute | solution.py:193
  43.3 0.9 copy-start.1
  46.5 24.0 %all-to-all-start.1 = ((bf16[32,4,16,224]{3,2,1,0:T(8,128)(2,1)}), bf16[32,4,16,224]{3,2,1,0:T(8,128)(2,1)S(1)}, u32[]{:S(2)}, u32[]{:S(2)}) async-start(bf16[32,4,16,224]{3,2,1,0:T(8,128)(2,1)} %pick.1), calls=%async_computation.1 | async-start | bytes 2097152 | tf_op jit(solution)/shard_map/all_to_all | solution.py:211
  71.1 37.9 %copy-start = (bf16[2,896,512]{2,1,0:T(8,128)(2,1)S(1)}, bf16[2,896,512]{2,1,0:T(8,128)(2,1)}, u32[]{:S(2)}) copy-start(bf16[2,896,512]{2,1,0:T(8,128)(2,1)} %kv_ref.1) | copy-start | bytes 5505028
  71.1 37.8 %copy-start.2 = (bf16[128,512]{1,0:T(8,128)(2,1)S(1)}, bf16[128,512]{1,0:T(8,128)(2,1)}, u32[]{:S(2)}) copy-start(bf16[128,512]{1,0:T(8,128)(2,1)} %q_ref.1) | copy-start | bytes 393220
  71.1 69.6 %all-to-all-start.2 = ((bf16[16,256,512]{2,1,0:T(8,128)(2,1)}), bf16[16,256,512]{2,1,0:T(8,128)(2,1)}, u32[]{:S(2)}, u32[]{:S(2)}) async-start(bf16[16,256,512]{2,1,0:T(8,128)(2,1)} %broadcast_in_dim.30), calls=%async_computation.2 | async-start | bytes 8388608 | tf_op jit(solution)/shard_map/all_to_all | solution.py:220
